TPU v7x, 128 devices: a whole 4x4x4 slice. The times are simulated.
128 devices in a mesh: term: 8 (over y, core), doc: 16 (over x, z).
Axes of the slice: x: 4, y: 4, z: 4, core: 2. Of those that a mesh axis runs over, the one named last changes fastest.
Arguments:
- doc_tiles: bfloat16 [8, 8192, 128, 128], P('term', 'doc'), may hold values from 0.049804688 to 3
- tile_rows: int32 [8, 8192], P('term', 'doc'), may hold values from 0 to 31
- tile_cols: int32 [8, 8192], P('term', 'doc'), may hold values from 0 to 511, as said below
- tile_count: int32 [8, 16], P('term', 'doc'), may hold values from 170 to 512, as said below
- factor_h: bfloat16 [128, 65536], P(None, ('term', 'doc')), may hold values from 0.049804688 to 1
- factor_w: float32 [32768, 128], P(('term', 'doc')), as said below
Outputs:
- new_w: float32 [32768, 128], P(('term', 'doc'))
Inputs may be any that keep to these rules, and one draw needn't show every extreme that they name: Device (i, j) uses only the first tile_count[i, j] entries of its list of 512; some device's count is exactly 512. `tile_rows`: coordinates may repeat within a stripe; repeated tiles add. `tile_cols`: device (i, j)'s tiles belong to document shard j: every column block c in its list has (c // 4) % 16 == j, that is, c lies in the document columns that factor_h keeps on the devices (0, j), (1, j), ..., (7, j). `factor_w`: positive entries.
All inputs are finite; a program needn't handle non-finite values.
Results may differ from a plain program's by a relative error of at most 0.0003.
Values may be sent and summed in bfloat16 or wider, within the bound.
No kernel may reach another device: no remote copies, remote signals or barrier semaphores. Data moves between devices by JAX's collectives and lax.ppermute only.
A program may use at most 192 MiB of HBM per device.

v0:
```python
import jax
import jax.numpy as jnp
from jax import lax
from jax.sharding import PartitionSpec as P


def hals_sweep(w_rows, cross_rows, gram):
    w_cols = w_rows.T
    a_cols = cross_rows.T
    rank = gram.shape[0]
    width = min(16, rank)

    def update_block(index, current):
        first = index * width
        g_rows = lax.dynamic_slice_in_dim(gram, first, width, 0)
        projected = jnp.dot(g_rows, current, precision=lax.Precision.HIGHEST)
        old_block = lax.dynamic_slice_in_dim(current, first, width, 0)
        a_block = lax.dynamic_slice_in_dim(a_cols, first, width, 0)
        g_square = lax.dynamic_slice_in_dim(g_rows, first, width, 1)
        changes = []
        fresh_rows = []
        for column in range(width):
            estimate = projected[column]
            for earlier in range(column):
                estimate = estimate + g_square[column, earlier] * changes[earlier]
            fresh = jnp.maximum(
                old_block[column] + (a_block[column] - estimate) / g_square[column, column], 0.0
            )
            changes.append(fresh - old_block[column])
            fresh_rows.append(fresh)
        return lax.dynamic_update_slice_in_dim(current, jnp.stack(fresh_rows, axis=0), first, 0)

    return lax.fori_loop(0, rank // width, update_block, w_cols).T


def self_gram(matrix):
    return lax.dot_general(
        matrix, matrix, (((1,), (1,)), ((), ())), preferred_element_type=jnp.float32
    )


def body(doc_tiles, tile_rows, tile_cols, tile_count, factor_h, factor_w):
    doc_count = lax.axis_size("doc")
    term_count = lax.axis_size("term")
    slots = doc_tiles.shape[1]
    tile_size = doc_tiles.shape[2]
    rank = factor_h.shape[0]
    own_rows = factor_w.shape[0]
    row_blocks = own_rows * doc_count // tile_size
    per_shard = factor_h.shape[1] // tile_size
    columns = tile_cols[0]
    gathered = lax.all_gather(factor_h, "term", axis=1, tiled=True)
    block_index = columns // per_shard // doc_count * per_shard + columns % per_shard
    gram = lax.psum(self_gram(factor_h), ("term", "doc"))
    h_blocks = gathered.reshape(rank, -1, tile_size)
    picked = jnp.take(h_blocks, block_index, axis=1)
    products = jnp.einsum("btd,kbd->btk", doc_tiles[0], picked, preferred_element_type=jnp.float32)
    live_mask = (jnp.arange(slots, dtype=jnp.int32) < tile_count[0, 0]).astype(jnp.float32)
    products = products * live_mask[:, None, None]
    stripe_part = jax.ops.segment_sum(products, tile_rows[0], num_segments=row_blocks)
    stripe_part = stripe_part.reshape(row_blocks * tile_size, rank)
    cross_rows = lax.psum_scatter(stripe_part, "doc", scatter_dimension=0, tiled=True)
    updated = hals_sweep(factor_w, cross_rows, gram)
    squares = lax.psum(jnp.sum(updated * updated, axis=0), ("term", "doc"))
    all_rows = own_rows * term_count * doc_count
    rms = jnp.sqrt(squares / all_rows + 1e-06)
    return updated / rms


def solution(mesh):
    in_specs = (
        P("term", "doc", None, None),
        P("term", "doc"),
        P("term", "doc"),
        P("term", "doc"),
        P(None, ("term", "doc")),
        P(("term", "doc"), None),
    )
    out_specs = P(("term", "doc"), None)
    return jax.shard_map(body, mesh=mesh, in_specs=in_specs, out_specs=out_specs, check_vma=False)
```

profile of v0, /device:TPU:1, one launch (start us, length us, event | category | flops | bytes accessed | tf_op | source)
XLA Modules:
  0.0 1078.1 jit_solution(14901425534949723841)
XLA Ops:
  13.1 23.9 %all-gather.2.cloned.1.call-done = bf16[128,4096]{0,1:T(8,128)(2,1)} async-done(((bf16[128,512]{0,1:T(8,128)(2,1)}), bf16[128,4096]{0,1:T(8,128)(2,1)}) %all-gather.2.cloned.1.call-update) | async-done | bytes 1048592 | tf_op jit(solution)/shard_map/all_gather | solution.py:52
  38.6 13.9 %gather_fusion = bf16[512,128,128]{2,1,0:T(8,128)(2,1)} fusion(bf16[128,32,128]{2,0,1:T(8,128)(2,1)S(1)} %copy.17, s32[1024]{0:T(1024)S(1)} %pad_clamp_fusion), kind=kCustom, calls=%fused_computation | custom fusion | bytes 33556480 | tf_op jit(solution)/shard_map/jit(_take)/gather | solution.py:56
  52.4 26.0 %multiply_bitcast_fusion = f32[512,128,128]{1,2,0:T(8,128)} fusion(f32[512]{0:T(512)S(1)} %get-tuple-element.303, bf16[1,512,128,128]{3,2,1,0:T(8,128)(2,1)} %param.8, bf16[512,128,128]{2,1,0:T(8,128)(2,1)} %gather_fusion, pred[512]{0:T(512)(128)(4,1)S(1)} %get-tuple-element.304), kind=kOutput, calls=%fused_computation.141 | convolution fusion | flops 2164260864 | bytes 67111424 | tf_op jit(solution)/shard_map/btd,kbd->btk/dot_general | solution.py:57
  78.4 33.5 %copy.18 = f32[512,128,128]{2,1,0:T(8,128)} copy(f32[512,128,128]{1,2,0:T(8,128)} %multiply_bitcast_fusion) | data formatting | bytes 67108864 | tf_op jit(solution)/shard_map/mul | solution.py:59
  112.1 66.1 %scatter_fusion = f32[32,128,128]{2,1,0:T(8,128)S(1)} fusion(f32[32,128,128]{2,1,0:T(8,128)S(1)} %broadcast_in_dim.15, s32[512]{0:T(512)S(1)} %bitcast.457, f32[512,128,128]{2,1,0:T(8,128)} %copy.18), kind=kCustom, calls=%fused_computation.1 | custom fusion | flops 8388608 | bytes 100665344 | tf_op jit(solution)/shard_map/scatter-add | solution.py:60
  180.3 72.2 %reduce-scatter.2.cloned.1.call-done = f32[256,128]{0,1:T(8,128)} async-done(((f32[4096,128]{0,1:T(8,128)}), f32[256,128]{0,1:T(8,128)}) %reduce-scatter.2.cloned.1.call-update) | async-done | bytes 131088 | tf_op jit(solution)/shard_map/reduce_scatter | solution.py:62
  252.5 751.5 %while.16 = (s32[]{:T(128)}, f32[128,256]{1,0:T(8,128)S(1)}, f32[128,256]{1,0:T(8,128)}, f32[128,128]{1,0:T(8,128)}, s32[]{:T(128)}, /*index=5*/s32[]{:T(128)}, ...) while((s32[]{:T(128)}, f32[128,256]{1,0:T(8,128)S(1)}, ...), condition=%wide.region_4.5_spmd, body=%wide.region_3.4_spmd.sunk | while | flops 6373157 | bytes 315747 | solution.py:33
  258.9 57.9 %fusion.132 = (f32[1,256]{1,0:T(1,128)S(1)}, f32[1,256]{1,0:T(1,128)S(1)}, f32[1,256]{1,0:T(1,128)S(1)}, f32[1,256]{1,0:T(1,128)S(1)}, f32[1,256]{1,0:T(1,128)S(...) fusion(f32[128,256]{1,0:T(8,128)S(1)} %get-tuple-element.685, ...), kind=kLoop, calls=%fused_computation.139.clone.1 | loop fusion | flops 56576 | bytes 66976 | tf_op jit(solution)/shard_map/while/body/eval_jaxpr/sub | solution.py:29
  316.8 29.0 %fusion.133 = (f32[1,256]{1,0:T(1,128)S(1)}, f32[1,256]{1,0:T(1,128)S(1)}, f32[1,256]{1,0:T(1,128)S(1)}) fusion(f32[1,256]{1,0:T(1,128)S(1)} %get-tuple-element.599, f32[1,256]{1,0:T(1,128)S(1)} %get-tuple-element.600, f32[1,256]{1,0:T(1,128)S(1)} %get-tuple-element.601, f32[1,256]{1,0:T(1,128)S(1)} %get-tuple-element.602, ...), kind=kLoop, calls=%fused_computation.126.clone.1 | loop fusion | flops 25088 | bytes 25792 | tf_op jit(solution)/shard_map/while/body/eval_jaxpr/max | solution.py:26
  352.9 57.9 %fusion.132 = (f32[1,256]{1,0:T(1,128)S(1)}, f32[1,256]{1,0:T(1,128)S(1)}, f32[1,256]{1,0:T(1,128)S(1)}, f32[1,256]{1,0:T(1,128)S(1)}, f32[1,256]{1,0:T(1,128)S(...) fusion(f32[128,256]{1,0:T(8,128)S(1)} %get-tuple-element.685, ...), kind=kLoop, calls=%fused_computation.139.clone.1 | loop fusion | flops 56576 | bytes 66976 | tf_op jit(solution)/shard_map/while/body/eval_jaxpr/sub | solution.py:29
  410.9 29.0 %fusion.133 = (f32[1,256]{1,0:T(1,128)S(1)}, f32[1,256]{1,0:T(1,128)S(1)}, f32[1,256]{1,0:T(1,128)S(1)}) fusion(f32[1,256]{1,0:T(1,128)S(1)} %get-tuple-element.599, f32[1,256]{1,0:T(1,128)S(1)} %get-tuple-element.600, f32[1,256]{1,0:T(1,128)S(1)} %get-tuple-element.601, f32[1,256]{1,0:T(1,128)S(1)} %get-tuple-element.602, ...), kind=kLoop, calls=%fused_computation.126.clone.1 | loop fusion | flops 25088 | bytes 25792 | tf_op jit(solution)/shard_map/while/body/eval_jaxpr/max | solution.py:26
  446.9 57.9 %fusion.132 = (f32[1,256]{1,0:T(1,128)S(1)}, f32[1,256]{1,0:T(1,128)S(1)}, f32[1,256]{1,0:T(1,128)S(1)}, f32[1,256]{1,0:T(1,128)S(1)}, f32[1,256]{1,0:T(1,128)S(...) fusion(f32[128,256]{1,0:T(8,128)S(1)} %get-tuple-element.685, ...), kind=kLoop, calls=%fused_computation.139.clone.1 | loop fusion | flops 56576 | bytes 66976 | tf_op jit(solution)/shard_map/while/body/eval_jaxpr/sub | solution.py:29
  504.9 29.0 %fusion.133 = (f32[1,256]{1,0:T(1,128)S(1)}, f32[1,256]{1,0:T(1,128)S(1)}, f32[1,256]{1,0:T(1,128)S(1)}) fusion(f32[1,256]{1,0:T(1,128)S(1)} %get-tuple-element.599, f32[1,256]{1,0:T(1,128)S(1)} %get-tuple-element.600, f32[1,256]{1,0:T(1,128)S(1)} %get-tuple-element.601, f32[1,256]{1,0:T(1,128)S(1)} %get-tuple-element.602, ...), kind=kLoop, calls=%fused_computation.126.clone.1 | loop fusion | flops 25088 | bytes 25792 | tf_op jit(solution)/shard_map/while/body/eval_jaxpr/max | solution.py:26
  540.9 57.9 %fusion.132 = (f32[1,256]{1,0:T(1,128)S(1)}, f32[1,256]{1,0:T(1,128)S(1)}, f32[1,256]{1,0:T(1,128)S(1)}, f32[1,256]{1,0:T(1,128)S(1)}, f32[1,256]{1,0:T(1,128)S(...) fusion(f32[128,256]{1,0:T(8,128)S(1)} %get-tuple-element.685, ...), kind=kLoop, calls=%fused_computation.139.clone.1 | loop fusion | flops 56576 | bytes 66976 | tf_op jit(solution)/shard_map/while/body/eval_jaxpr/sub | solution.py:29
  598.9 29.0 %fusion.133 = (f32[1,256]{1,0:T(1,128)S(1)}, f32[1,256]{1,0:T(1,128)S(1)}, f32[1,256]{1,0:T(1,128)S(1)}) fusion(f32[1,256]{1,0:T(1,128)S(1)} %get-tuple-element.599, f32[1,256]{1,0:T(1,128)S(1)} %get-tuple-element.600, f32[1,256]{1,0:T(1,128)S(1)} %get-tuple-element.601, f32[1,256]{1,0:T(1,128)S(1)} %get-tuple-element.602, ...), kind=kLoop, calls=%fused_computation.126.clone.1 | loop fusion | flops 25088 | bytes 25792 | tf_op jit(solution)/shard_map/while/body/eval_jaxpr/max | solution.py:26
  634.9 58.0 %fusion.132 = (f32[1,256]{1,0:T(1,128)S(1)}, f32[1,256]{1,0:T(1,128)S(1)}, f32[1,256]{1,0:T(1,128)S(1)}, f32[1,256]{1,0:T(1,128)S(1)}, f32[1,256]{1,0:T(1,128)S(...) fusion(f32[128,256]{1,0:T(8,128)S(1)} %get-tuple-element.685, ...), kind=kLoop, calls=%fused_computation.139.clone.1 | loop fusion | flops 56576 | bytes 66976 | tf_op jit(solution)/shard_map/while/body/eval_jaxpr/sub | solution.py:29
  692.9 29.0 %fusion.133 = (f32[1,256]{1,0:T(1,128)S(1)}, f32[1,256]{1,0:T(1,128)S(1)}, f32[1,256]{1,0:T(1,128)S(1)}) fusion(f32[1,256]{1,0:T(1,128)S(1)} %get-tuple-element.599, f32[1,256]{1,0:T(1,128)S(1)} %get-tuple-element.600, f32[1,256]{1,0:T(1,128)S(1)} %get-tuple-element.601, f32[1,256]{1,0:T(1,128)S(1)} %get-tuple-element.602, ...), kind=kLoop, calls=%fused_computation.126.clone.1 | loop fusion | flops 25088 | bytes 25792 | tf_op jit(solution)/shard_map/while/body/eval_jaxpr/max | solution.py:26
  729.0 57.9 %fusion.132 = (f32[1,256]{1,0:T(1,128)S(1)}, f32[1,256]{1,0:T(1,128)S(1)}, f32[1,256]{1,0:T(1,128)S(1)}, f32[1,256]{1,0:T(1,128)S(1)}, f32[1,256]{1,0:T(1,128)S(...) fusion(f32[128,256]{1,0:T(8,128)S(1)} %get-tuple-element.685, ...), kind=kLoop, calls=%fused_computation.139.clone.1 | loop fusion | flops 56576 | bytes 66976 | tf_op jit(solution)/shard_map/while/body/eval_jaxpr/sub | solution.py:29
  786.9 29.0 %fusion.133 = (f32[1,256]{1,0:T(1,128)S(1)}, f32[1,256]{1,0:T(1,128)S(1)}, f32[1,256]{1,0:T(1,128)S(1)}) fusion(f32[1,256]{1,0:T(1,128)S(1)} %get-tuple-element.599, f32[1,256]{1,0:T(1,128)S(1)} %get-tuple-element.600, f32[1,256]{1,0:T(1,128)S(1)} %get-tuple-element.601, f32[1,256]{1,0:T(1,128)S(1)} %get-tuple-element.602, ...), kind=kLoop, calls=%fused_computation.126.clone.1 | loop fusion | flops 25088 | bytes 25792 | tf_op jit(solution)/shard_map/while/body/eval_jaxpr/max | solution.py:26
  823.0 57.9 %fusion.132 = (f32[1,256]{1,0:T(1,128)S(1)}, f32[1,256]{1,0:T(1,128)S(1)}, f32[1,256]{1,0:T(1,128)S(1)}, f32[1,256]{1,0:T(1,128)S(1)}, f32[1,256]{1,0:T(1,128)S(...) fusion(f32[128,256]{1,0:T(8,128)S(1)} %get-tuple-element.685, ...), kind=kLoop, calls=%fused_computation.139.clone.1 | loop fusion | flops 56576 | bytes 66976 | tf_op jit(solution)/shard_map/while/body/eval_jaxpr/sub | solution.py:29
  880.9 29.0 %fusion.133 = (f32[1,256]{1,0:T(1,128)S(1)}, f32[1,256]{1,0:T(1,128)S(1)}, f32[1,256]{1,0:T(1,128)S(1)}) fusion(f32[1,256]{1,0:T(1,128)S(1)} %get-tuple-element.599, f32[1,256]{1,0:T(1,128)S(1)} %get-tuple-element.600, f32[1,256]{1,0:T(1,128)S(1)} %get-tuple-element.601, f32[1,256]{1,0:T(1,128)S(1)} %get-tuple-element.602, ...), kind=kLoop, calls=%fused_computation.126.clone.1 | loop fusion | flops 25088 | bytes 25792 | tf_op jit(solution)/shard_map/while/body/eval_jaxpr/max | solution.py:26
  917.0 57.9 %fusion.132 = (f32[1,256]{1,0:T(1,128)S(1)}, f32[1,256]{1,0:T(1,128)S(1)}, f32[1,256]{1,0:T(1,128)S(1)}, f32[1,256]{1,0:T(1,128)S(1)}, f32[1,256]{1,0:T(1,128)S(...) fusion(f32[128,256]{1,0:T(8,128)S(1)} %get-tuple-element.685, ...), kind=kLoop, calls=%fused_computation.139.clone.1 | loop fusion | flops 56576 | bytes 66976 | tf_op jit(solution)/shard_map/while/body/eval_jaxpr/sub | solution.py:29
  974.9 29.0 %fusion.133 = (f32[1,256]{1,0:T(1,128)S(1)}, f32[1,256]{1,0:T(1,128)S(1)}, f32[1,256]{1,0:T(1,128)S(1)}) fusion(f32[1,256]{1,0:T(1,128)S(1)} %get-tuple-element.599, f32[1,256]{1,0:T(1,128)S(1)} %get-tuple-element.600, f32[1,256]{1,0:T(1,128)S(1)} %get-tuple-element.601, f32[1,256]{1,0:T(1,128)S(1)} %get-tuple-element.602, ...), kind=kLoop, calls=%fused_computation.126.clone.1 | loop fusion | flops 25088 | bytes 25792 | tf_op jit(solution)/shard_map/while/body/eval_jaxpr/max | solution.py:26
  1004.1 65.9 %psum.15 = f32[128]{0:T(128)S(1)} all-reduce(f32[128]{0:T(128)S(1)} %multiply_reduce_fusion), channel_id=1, replica_groups=mesh['term'=8,'doc'=16] {'term','doc'}, use_global_device_ids=true, to_apply=%region_6.7 | all-reduce | flops 128 | bytes 1024 | tf_op jit(solution)/shard_map/psum | solution.py:64
  (56 shorter events, 65.6 us)
Async XLA Ops:
  7.4 29.6 %all-gather.2.cloned.1.call-start = ((), (), s32[]{:S(2)}) async-start(), calls=%async_computation.1 | async-start | bytes 1179648 | tf_op jit(solution)/shard_map/all_gather | solution.py:52
  9.1 171.2 %all-reduce.2.cloned.1.call-start = ((), (), s32[]{:S(2)}) async-start(), calls=%async_computation.3 | async-start | bytes 131072 | tf_op jit(solution)/shard_map/psum | solution.py:54
  10.9 241.5 %reduce-scatter.2.cloned.1.call-start = ((), (), s32[]{:S(2)}) async-start(), calls=%async_computation.2 | async-start | bytes 2228224 | tf_op jit(solution)/shard_map/reduce_scatter | solution.py:62
  78.4 33.7 %copy-start.1 = (s32[1,512]{1,0:T(1,128)S(1)}, s32[1,512]{1,0:T(1,128)}, u32[]{:S(2)}) copy-start(s32[1,512]{1,0:T(1,128)} %param.9) | copy-start | bytes 6148
  112.1 68.0 %copy-start = (f32[256,128]{1,0:T(8,128)S(1)}, f32[256,128]{1,0:T(8,128)}, u32[]{:S(2)}) copy-start(f32[256,128]{1,0:T(8,128)} %param.13) | copy-start | bytes 393220
Sparse Core Ops, SparseCore 0:
  9.9 26.9 all-gather.1
  180.2 72.1 reduce-scatter.1
Sparse Core Ops, SparseCore 1:
  15.0 141.9 all-reduce.1
where the time goes:
time: 1090 us; the launch traced here: 1080 us
  other arithmetic  764 us (70%)
  local copies, waits for them, and re-layouts  102 us (9%)
  waiting for transfers between devices  96.2 us (9%)
  blocking collectives  65.9 us (6%)
  matrix products  34.6 us (3%)
  between operations  15.6 us (1%)
    sub x8, other arithmetic, update_block(): changes.append(fresh - old_block[column])  464 us
    max x8, other arithmetic, update_block(): jnp.maximum(old_block[column] + (a_block[column] - estimate) / g_square[c...  232 us
    reduce_scatter x1, waiting for transfers between devices, body(): lax.psum_scatter(stripe_part, 'doc', scatter_dimension=0, tiled=True)  72.2 us
    scatter-add x1, other arithmetic, body(): jax.ops.segment_sum(products, tile_rows[0], num_segments=row_blocks)  66.1 us
    psum x1, blocking collectives, body(): squares = lax.psum(jnp.sum(updated * updated, axis=0), ('term', 'doc'))  65.9 us
    slice x8, local copies, waits for them, and re-layouts, update_block(): estimate = estimate + g_square[column, earlier] * changes[earlier]  48.5 us
    mul x1, local copies, waits for them, and re-layouts, body(): products = products * live_mask[:, None, None]  33.5 us
    dot_general x1, matrix products, body(): jnp.einsum('btd,kbd->btk', doc_tiles[0], picked, preferred_element_type=j...  26 us
  transfers between devices with their start and end apart: 3, of which 2 were waited for; matrix products, arithmetic and copies ran while one was open for 14% of the time, Pallas kernels for 0%

commit v1 on v0

v1 whole, which is shorter than its diff:
```python
import jax
import jax.numpy as jnp
from jax import lax
from jax.experimental import pallas as pl
from jax.experimental.pallas import tpu as pltpu
from jax.sharding import PartitionSpec as P

CHUNK = 32
UNROLL = 4
ANY = pl.ANY
VMEM = pltpu.VMEM
SMEM = pltpu.SMEM


def along_y(x, step):
    return lax.ppermute(x, "term", [(i, (i + 2 * step) % 8) for i in range(8)])


def other_core(x):
    return lax.ppermute(x, "term", [(i, i ^ 1) for i in range(8)])


def products_kernel(rows, blocks, count, near, far, tiles, out, held, h_all, sems):
    live = count[0]
    chunks = pl.cdiv(live, CHUNK)

    def fetch(c):
        part = pl.ds(c * CHUNK, CHUNK)
        return pltpu.make_async_copy(tiles.at[part], held.at[part], sems.at[c])

    @pl.loop(0, chunks)
    def _(c):
        fetch(c).start()

    out[...] = jnp.zeros_like(out)
    for s in range(4):
        for b in range(4):
            h_all[s * 4 + b] = near[s, b * 128 : (b + 1) * 128, :]
            h_all[16 + s * 4 + b] = far[s, b * 128 : (b + 1) * 128, :]
    h_all[32] = jnp.zeros((128, 128), jnp.bfloat16)

    @pl.loop(0, chunks)
    def _(c):
        fetch(c).wait()

        @pl.loop(0, CHUNK // UNROLL)
        def _(step):
            first = c * CHUNK + step * UNROLL
            found = []
            for u in range(UNROLL):
                e = first + u
                block = jnp.where(e < live, blocks[e], 32)
                found.append(jnp.dot(held[e], h_all[block], preferred_element_type=jnp.float32))
            for u in range(UNROLL):
                row = rows[first + u]
                out[row] += found[u]


def tile_products(rows, blocks, count, near, far, tiles):
    return pl.pallas_call(
        products_kernel,
        out_shape=jax.ShapeDtypeStruct((32, 128, 128), jnp.float32),
        in_specs=[pl.BlockSpec(memory_space=SMEM)] * 3
        + [pl.BlockSpec(memory_space=VMEM)] * 2
        + [pl.BlockSpec(memory_space=ANY)],
        out_specs=pl.BlockSpec(memory_space=VMEM),
        scratch_shapes=[
            VMEM((512, 128, 128), jnp.bfloat16),
            VMEM((33, 128, 128), jnp.bfloat16),
            pltpu.SemaphoreType.DMA((512 // CHUNK,)),
        ],
        compiler_params=pltpu.CompilerParams(vmem_limit_bytes=40 * 2**20),
    )(rows, blocks, count, near, far, tiles)


def sweep_kernel(parts, grams, w, fresh, squares):
    gram = grams[0]
    cross = parts[0]
    for j in range(1, 16):
        gram = gram + grams[j]
        cross = cross + parts[j]
    row_id = lax.broadcasted_iota(jnp.int32, (128, 128), 0)
    col_id = lax.broadcasted_iota(jnp.int32, (128, 128), 1)
    diagonal = jnp.sum(jnp.where(row_id == col_id, gram, 0.0), axis=1, keepdims=True)
    inverse = 1.0 / diagonal
    w_t = w[...].T
    rest = cross.T - jnp.dot(
        gram, w_t, precision=lax.Precision.HIGHEST, preferred_element_type=jnp.float32
    )
    estimate = w_t + rest * inverse
    scaled = jnp.where(col_id < row_id, gram * inverse, 0.0)
    groups = [estimate[8 * q : 8 * q + 8] for q in range(16)]
    for k in range(128):
        q, s = divmod(k, 8)
        change = jnp.maximum(groups[q][s : s + 1], 0.0) - w_t[k : k + 1]
        for later in range(q, 16):
            groups[later] = groups[later] - scaled[8 * later : 8 * later + 8, k : k + 1] * change
    updated = jnp.maximum(jnp.concatenate(groups, axis=0), 0.0).T
    fresh[...] = updated
    squares[...] = jnp.sum(updated * updated, axis=0, keepdims=True)


def sweep(parts, grams, w):
    return pl.pallas_call(
        sweep_kernel,
        out_shape=(
            jax.ShapeDtypeStruct((256, 128), jnp.float32),
            jax.ShapeDtypeStruct((1, 128), jnp.float32),
        ),
        in_specs=[pl.BlockSpec(memory_space=VMEM)] * 3,
        out_specs=[pl.BlockSpec(memory_space=VMEM)] * 2,
        compiler_params=pltpu.CompilerParams(vmem_limit_bytes=32 * 2**20),
    )(parts, grams, w)


def scale_kernel(total_rows, squares, updated, out):
    total = jnp.sum(squares[...], axis=0, keepdims=True)
    rms = jnp.sqrt(total / total_rows + 1e-06)
    out[...] = updated[...] / rms


def scale(squares, updated, total_rows):
    def kernel(*refs):
        scale_kernel(total_rows, *refs)

    return pl.pallas_call(
        kernel,
        out_shape=jax.ShapeDtypeStruct(updated.shape, jnp.float32),
    )(squares, updated)


def body(doc_tiles, tile_rows, tile_cols, tile_count, factor_h, factor_w):
    me = lax.axis_index("term")
    own = factor_h.T
    near = jnp.stack([own] + [along_y(own, s) for s in (1, 2, 3)])
    far = other_core(near)
    columns = tile_cols[0]
    owner = columns // 64
    blocks = (me // 2 - owner // 2) % 4 * 4 + columns % 4
    blocks = blocks + jnp.where(owner % 2 == me % 2, 0, 16)

    def self_gram(x):
        x = x.reshape(-1, 128)
        return lax.dot_general(x, x, (((0,), (0,)), ((), ())), preferred_element_type=jnp.float32)

    gram = self_gram(near) + self_gram(far)
    grams = lax.all_to_all(jnp.broadcast_to(gram, (16, 128, 128)), "doc", 0, 0)
    partial = tile_products(tile_rows[0], blocks, tile_count[0], near, far, doc_tiles[0])
    parts = lax.all_to_all(partial.reshape(16, 256, 128), "doc", 0, 0)
    updated, squares = sweep(parts, grams, factor_w)
    shared = lax.all_to_all(jnp.broadcast_to(squares, (128, 1, 128)), ("term", "doc"), 0, 0)
    return scale(shared.reshape(128, 128), updated, 32768)


def solution(mesh):
    in_specs = (
        P("term", "doc", None, None),
        P("term", "doc"),
        P("term", "doc"),
        P("term", "doc"),
        P(None, ("term", "doc")),
        P(("term", "doc"), None),
    )
    out_specs = P(("term", "doc"), None)
    return jax.shard_map(body, mesh=mesh, in_specs=in_specs, out_specs=out_specs, check_vma=False)
```

time: 1090 us -> 106 us (0.10); the launches traced: 1080 us -> 105 us
  other arithmetic: 764 us -> 0.1 us
  local copies, waits for them, and re-layouts: 102 us -> 2.84 us
  waiting for transfers between devices: 96.2 us -> 5.14 us
  matrix products: 34.6 us -> 0.68 us
  Pallas kernels: 0 us -> 24.5 us
  starting transfers between devices: 0.09 us -> 15.6 us
  between operations: 15.6 us -> 0.77 us
    sub x8 -> x0, other arithmetic: 464 us -> none  [update_block(): changes.append(fresh - old_block[column])]
    max x8 -> x0, other arithmetic: 232 us -> none  [update_block(): jnp.maximum(old_block[column] + (a_block[column] - estimate) / g_square[c...]
    reduce_scatter x1 -> x0, waiting for transfers between devices: 72.2 us -> none  [body(): lax.psum_scatter(stripe_part, 'doc', scatter_dimension=0, tiled=True)]
    scatter-add x1 -> x0, other arithmetic: 66.1 us -> none  [body(): jax.ops.segment_sum(products, tile_rows[0], num_segments=row_blocks)]
    psum x1 -> x0, blocking collectives: 65.9 us -> none  [body(): squares = lax.psum(jnp.sum(updated * updated, axis=0), ('term', 'doc'))]
    all_to_all x0 -> x2, blocking collectives: none -> 55.7 us  [the longest x1 38.6 us: body(): parts = lax.all_to_all(partial.reshape(16, 256, 128), 'doc', 0, 0)]
    slice x8 -> x0, local copies, waits for them, and re-layouts: 48.5 us -> none  [update_block(): estimate = estimate + g_square[column, earlier] * changes[earlier]]
    dot_general x10 -> x2, matrix products: 34.6 us -> 0.68 us  [self_gram(): lax.dot_general(x, x, (((0,), (0,)), ((), ())), preferred_element_type=jn...]
  transfers between devices with their start and end apart: 3 -> 5, of which waited for: 2 -> 3; matrix products, arithmetic and copies ran while one was open for 14% -> 0% of each run, Pallas kernels for 0% -> 19%
where the time goes in v1:
time: 106 us; the launch traced here: 105 us
  blocking collectives  55.7 us (53%)
  Pallas kernels  24.5 us (23%)
  starting transfers between devices  15.6 us (15%)
  waiting for transfers between devices  5.14 us (5%)
  local copies, waits for them, and re-layouts  2.84 us (3%)
    all_to_all x1, blocking collectives, body(): parts = lax.all_to_all(partial.reshape(16, 256, 128), 'doc', 0, 0)  38.6 us
    pallas_call x1, Pallas kernels, tile_products(): pl.pallas_call(products_kernel, out_shape=jax.ShapeDtypeStruct((32, 128,...  19.8 us
    all_to_all x1, blocking collectives, body(): lax.all_to_all(jnp.broadcast_to(squares, (128, 1, 128)), ('term', 'doc'),...  17.1 us
    all_to_all x1, starting transfers between devices, body(): grams = lax.all_to_all(jnp.broadcast_to(gram, (16, 128, 128)), 'doc', 0, 0)  7.69 us
    ppermute x3, starting transfers between devices, along_y(): return lax.ppermute(x, 'term', [(i, (i + 2 * step) % 8) for i in range(8)])  6.5 us
    ppermute x3, waiting for transfers between devices, along_y(): return lax.ppermute(x, 'term', [(i, (i + 2 * step) % 8) for i in range(8)])  3.6 us
    pallas_call x1, Pallas kernels, sweep(): pl.pallas_call(sweep_kernel, out_shape=(jax.ShapeDtypeStruct((256, 128),...  3.02 us
  transfers between devices with their start and end apart: 5, of which 3 were waited for; matrix products, arithmetic and copies ran while one was open for 0% of the time, Pallas kernels for 19%

profile of v1, /device:TPU:1, one launch (start us, length us, event | category | flops | bytes accessed | tf_op | source)
XLA Modules:
  0.0 105.3 jit_solution(9330682838602148938)
XLA Ops:
  0.0 1.0 copy.10
  1.0 3.8 %collective-permute-start.1 = (bf16[512,128]{1,0:T(8,128)(2,1)S(1)}, bf16[512,128]{1,0:T(8,128)(2,1)S(1)}, u32[]{:S(2)}, u32[]{:S(2)}) collective-permute-start(bf16[512,128]{1,0:T(8,128)(2,1)S(1)} %bitcast.28), channel_id=1, source_target_pairs={{0,64},{16,80},{32,96},{48,112},{64,0},{80,16},{96,32},{112,48},{1... | collective-permute-start | bytes 393224 | tf_op jit(solution)/shard_map/ppermute | solution.py:16
  4.8 0.4 collective-permute-start
  5.2 2.3 %collective-permute-start.2 = (bf16[512,128]{1,0:T(8,128)(2,1)S(1)}, bf16[512,128]{1,0:T(8,128)(2,1)S(1)}, u32[]{:S(2)}, u32[]{:S(2)}) collective-permute-start(bf16[512,128]{1,0:T(8,128)(2,1)S(1)} %bitcast.30), channel_id=1, source_target_pairs={{0,96},{16,112},{32,0},{48,16},{64,32},{80,48},{96,64},{112,80},{1... | collective-permute-start | bytes 393224 | tf_op jit(solution)/shard_map/ppermute | solution.py:16
  7.5 0.3 collective-permute-done.1
  7.8 3.3 %collective-permute-done = bf16[512,128]{1,0:T(8,128)(2,1)S(1)} collective-permute-done((bf16[512,128]{1,0:T(8,128)(2,1)S(1)}, bf16[512,128]{1,0:T(8,128)(2,1)S(1)}, u32[]{:S(2)}, u32[]{:S(2)}) %collective-permute-start) | collective-permute-done | bytes 131104 | tf_op jit(solution)/shard_map/ppermute | solution.py:16
  11.1 0.0 collective-permute-done.2
  11.1 0.1 pad_maximum_fusion.near
  11.2 1.4 %collective-permute-start.3 = (bf16[4,512,128]{2,1,0:T(8,128)(2,1)S(1)}, bf16[4,512,128]{2,1,0:T(8,128)(2,1)S(1)}, u32[]{:S(2)}, u32[]{:S(2)}) collective-permute-start(bf16[4,512,128]{2,1,0:T(8,128)(2,1)S(1)} %pad_maximum_fusion.near), channel_id=1, source_target_pairs={{0,16},{16,0},{32,48},{48,32},{64,80},{80,64},{96,112},{112,96},{1... | collective-permute-start | bytes 1572872 | tf_op jit(solution)/shard_map/ppermute | solution.py:20
  12.7 1.5 %collective-permute-done.3.far = bf16[4,512,128]{2,1,0:T(8,128)(2,1)S(1)} collective-permute-done((bf16[4,512,128]{2,1,0:T(8,128)(2,1)S(1)}, bf16[4,512,128]{2,1,0:T(8,128)(2,1)S(1)}, u32[]{:S(2)}, u32[]{:S(2)}) %collective-permute-start.3) | collective-permute-done | bytes 524320 | tf_op jit(solution)/shard_map/ppermute | solution.py:20
  14.2 0.3 convolution_bitcast_fusion
  14.5 0.0 copy-start.3
  14.5 0.0 copy-start.2
  14.6 0.3 fusion
  14.9 1.1 %broadcast_in_dim.13 = f32[16,128,128]{2,1,0:T(8,128)} broadcast(f32[128,128]{1,0:T(8,128)S(1)} %fusion), dimensions={1,2} | broadcast | bytes 1114112 | tf_op jit(solution)/shard_map/broadcast_in_dim | solution.py:147
  16.0 7.7 %all-to-all-start.1 = ((f32[16,128,128]{2,1,0:T(8,128)}), f32[16,128,128]{2,1,0:T(8,128)}, u32[]{:S(2)}, u32[]{:S(2)}) async-start(f32[16,128,128]{2,1,0:T(8,128)} %broadcast_in_dim.13), calls=%async_computation.1 | async-start | bytes 2097152 | tf_op jit(solution)/shard_map/all_to_all | solution.py:147
  24.4 19.8 %shard_map.64 = f32[32,128,128]{2,1,0:T(8,128)S(1)} custom-call(s32[512]{0:T(512)S(1)} %bitcast.25, s32[512]{0:T(512)S(1)} %fusion.6.blocks, s32[1]{0:T(128)} %bitcast.23.count, bf16[4,512,128]{2,1,0:T(8,128)(2,1)S(1)} %pad_maximum_fusion.near, bf16[4,512,128]{2,1,0:T(8,128)(2,1)S(1)} %collective-permute-done.3.far, bf16[512,128,128]{2,1,0:T(8,128)(2,1)} %bitcast.27), custom_call_target="tpu_custom_call" | custom-call | tf_op jit(solution)/shard_map/pallas_call | solution.py:60
  44.2 0.0 all-to-all-done.1.grams
  44.3 0.0 copy-start
  44.3 38.6 %all_to_all.15.parts = f32[16,256,128]{2,1,0:T(8,128)S(1)} all-to-all(f32[16,256,128]{2,1,0:T(8,128)S(1)} %bitcast.24), channel_id=1, replica_groups=mesh['term'=8,'doc'=16] {'doc'}, dimensions={0} | all-to-all | bytes 4194304 | tf_op jit(solution)/shard_map/all_to_all | solution.py:149
  82.9 3.0 %shard_map.65 = (f32[256,128]{1,0:T(8,128)S(1)}, f32[1,128]{1,0:T(1,128)S(1)}) custom-call(f32[16,256,128]{2,1,0:T(8,128)S(1)} %all_to_all.15.parts, f32[16,128,128]{2,1,0:T(8,128)} %all-to-all-done.1.grams, f32[256,128]{1,0:T(8,128)S(1)} %copy-done), custom_call_target="tpu_custom_call" | custom-call | tf_op jit(solution)/shard_map/pallas_call | solution.py:104
  85.9 0.6 copy-done.1
  86.6 17.1 %all_to_all.16 = f32[128,1,128]{2,1,0:T(1,128)} all-to-all(f32[128,1,128]{2,1,0:T(1,128)S(1)} %broadcast_in_dim.14), channel_id=1, replica_groups=mesh['term'=8,'doc'=16] {'term','doc'}, dimensions={0} | all-to-all | bytes 131072 | tf_op jit(solution)/shard_map/all_to_all | solution.py:151
  103.7 1.6 %shard_map.66 = f32[256,128]{1,0:T(8,128)} custom-call(f32[128,128]{1,0:T(8,128)} %bitcast.32, f32[256,128]{1,0:T(8,128)} %copy-done.1), custom_call_target="tpu_custom_call" | custom-call | tf_op jit(solution)/shard_map/pallas_call | solution.py:126
  (6 shorter events, 0.1 us)
Async XLA Ops:
  1.0 6.8 %collective-permute-start.1 = (bf16[512,128]{1,0:T(8,128)(2,1)S(1)}, bf16[512,128]{1,0:T(8,128)(2,1)S(1)}, u32[]{:S(2)}, u32[]{:S(2)}) collective-permute-start(bf16[512,128]{1,0:T(8,128)(2,1)S(1)} %bitcast.28), channel_id=1, source_target_pairs={{0,64},{16,80},{32,96},{48,112},{64,0},{80,16},{96,32},{112,48},{1... | collective-permute-start | bytes 393224 | tf_op jit(solution)/shard_map/ppermute | solution.py:16
  4.8 6.3 %collective-permute-start = (bf16[512,128]{1,0:T(8,128)(2,1)S(1)}, bf16[512,128]{1,0:T(8,128)(2,1)S(1)}, u32[]{:S(2)}, u32[]{:S(2)}) collective-permute-start(bf16[512,128]{1,0:T(8,128)(2,1)S(1)} %bitcast.29), channel_id=1, source_target_pairs={{0,32},{16,48},{32,64},{48,80},{64,96},{80,112},{96,0},{112,16},{1... | collective-permute-start | bytes 393224 | tf_op jit(solution)/shard_map/ppermute | solution.py:16
  5.2 5.9 %collective-permute-start.2 = (bf16[512,128]{1,0:T(8,128)(2,1)S(1)}, bf16[512,128]{1,0:T(8,128)(2,1)S(1)}, u32[]{:S(2)}, u32[]{:S(2)}) collective-permute-start(bf16[512,128]{1,0:T(8,128)(2,1)S(1)} %bitcast.30), channel_id=1, source_target_pairs={{0,96},{16,112},{32,0},{48,16},{64,32},{80,48},{96,64},{112,80},{1... | collective-permute-start | bytes 393224 | tf_op jit(solution)/shard_map/ppermute | solution.py:16
  11.2 3.0 %collective-permute-start.3 = (bf16[4,512,128]{2,1,0:T(8,128)(2,1)S(1)}, bf16[4,512,128]{2,1,0:T(8,128)(2,1)S(1)}, u32[]{:S(2)}, u32[]{:S(2)}) collective-permute-start(bf16[4,512,128]{2,1,0:T(8,128)(2,1)S(1)} %pad_maximum_fusion.near), channel_id=1, source_target_pairs={{0,16},{16,0},{32,48},{48,32},{64,80},{80,64},{96,112},{112,96},{1... | collective-permute-start | bytes 1572872 | tf_op jit(solution)/shard_map/ppermute | solution.py:20
  14.5 9.9 %copy-start.3 = (s32[1,512]{1,0:T(1,128)S(1)}, s32[1,512]{1,0:T(1,128)}, u32[]{:S(2)}) copy-start(s32[1,512]{1,0:T(1,128)} %param.8) | copy-start | bytes 6148
  14.5 9.9 %copy-start.2 = (s32[1,512]{1,0:T(1,128)S(1)}, s32[1,512]{1,0:T(1,128)}, u32[]{:S(2)}) copy-start(s32[1,512]{1,0:T(1,128)} %param.7) | copy-start | bytes 6148
  16.0 28.2 %all-to-all-start.1 = ((f32[16,128,128]{2,1,0:T(8,128)}), f32[16,128,128]{2,1,0:T(8,128)}, u32[]{:S(2)}, u32[]{:S(2)}) async-start(f32[16,128,128]{2,1,0:T(8,128)} %broadcast_in_dim.13), calls=%async_computation.1 | async-start | bytes 2097152 | tf_op jit(solution)/shard_map/all_to_all | solution.py:147
  44.3 38.7 %copy-start = (f32[256,128]{1,0:T(8,128)S(1)}, f32[256,128]{1,0:T(8,128)}, u32[]{:S(2)}) copy-start(f32[256,128]{1,0:T(8,128)} %w.1) | copy-start | bytes 393220
  85.9 0.6 copy-start.1

commit v2 on v1

v2 whole, which is shorter than its diff:
```python
import functools

import jax
import jax.numpy as jnp
from jax import lax
from jax.experimental import pallas as pl
from jax.experimental.pallas import tpu as pltpu
from jax.sharding import PartitionSpec as P

UNROLL = 16
ANY = pl.ANY
VMEM = pltpu.VMEM
SMEM = pltpu.SMEM


def along_y(x, step):
    return lax.ppermute(x, "term", [(i, (i + 2 * step) % 8) for i in range(8)])


def other_core(x):
    return lax.ppermute(x, "term", [(i, i ^ 1) for i in range(8)])


def along_x(x, step):
    return lax.ppermute(x, "doc", [(i, (i + 4 * step) % 16) for i in range(16)])


def along_z(x, step):
    return lax.ppermute(x, "doc", [(i, i // 4 * 4 + (i + step) % 4) for i in range(16)])


def resident(x):
    return pltpu.with_memory_space_constraint(x, VMEM)


def plan_kernel(rows, columns, count, plan):
    live = count[0, 0]
    c = columns[...]
    block = c // 64 * 4 + c % 4 + 1
    slot = lax.broadcasted_iota(jnp.int32, (1, 512), 1)
    row = jnp.where(slot < live, rows[...], 127)
    value = (slot + 1024 * block + 65536 * (row // 2)).astype(jnp.float32)
    lane = lax.broadcasted_iota(jnp.int32, (128, 128), 1)
    line = lax.broadcasted_iota(jnp.int32, (128, 128), 0)

    def down(x, g):
        return jnp.broadcast_to(x[:, 128 * g : 128 * g + 128], (128, 128)).T

    before = (lane < line).astype(jnp.bfloat16)
    row_f = row.astype(jnp.float32)
    members, ranks, total = [], [], jnp.zeros((1, 128), jnp.float32)
    for g in range(4):
        member = ((lane == down(row_f, g).astype(jnp.int32)) & (lane < 32)).astype(jnp.float32)
        rank = jnp.dot(before, member.astype(jnp.bfloat16), preferred_element_type=jnp.float32)
        ranks.append(rank + total)
        members.append(member)
        total = total + jnp.sum(member, axis=0, keepdims=True)
    groups = jnp.floor((total + 3.0) * 0.25)
    odd = lane % 2
    starts = 4.0 * jnp.dot(
        jnp.broadcast_to(groups, (8, 128)).astype(jnp.bfloat16),
        ((line < lane) & (line % 2 == odd)).astype(jnp.bfloat16),
        preferred_element_type=jnp.float32,
    )[:1]
    starts = starts + 640.0 * odd[:1].astype(jnp.float32)
    found = [jnp.zeros((1, 128), jnp.float32)] * 10
    for g in range(4):
        position = jnp.sum(members[g] * (ranks[g] + starts), axis=1, keepdims=True)
        alive = jnp.sum(members[g], axis=1, keepdims=True)
        position = jnp.where(alive > 0.0, position, -1.0).astype(jnp.int32)
        values = down(value, g)
        for t in range(10):
            hit = jnp.where(position == lane + 128 * t, values, 0.0)
            found[t] = found[t] + jnp.sum(hit, axis=0, keepdims=True)
    for t in range(10):
        plan[t : t + 1] = found[t].astype(jnp.int32)
    for half in range(2):
        mine = jnp.where(odd[:1] == half, groups, 0.0)
        quads = jnp.sum(mine, axis=1, keepdims=True).astype(jnp.int32)
        plan[10 + half : 11 + half] = jnp.broadcast_to(quads, (1, 128))
    plan[12:16] = jnp.zeros((4, 128), jnp.int32)


def make_plan(rows, columns, count):
    return pl.pallas_call(
        plan_kernel,
        out_shape=jax.ShapeDtypeStruct((16, 128), jnp.int32),
        in_specs=[pl.BlockSpec(memory_space=VMEM)] * 2 + [pl.BlockSpec(memory_space=SMEM)],
        out_specs=pl.BlockSpec(memory_space=VMEM),
        cost_estimate=pl.CostEstimate(flops=10**8, bytes_accessed=10**5, transcendentals=0),
        compiler_params=pltpu.CompilerParams(vmem_limit_bytes=8 * 2**20),
    )(rows, columns, count)


def products_kernel(half, plan_in, near, far, gram, tiles, *refs):
    outs, (sums, h_all, plan, plan_sem) = refs[:4], refs[4:]
    plan_copy = pltpu.make_async_copy(plan_in, plan, plan_sem)
    plan_copy.start()
    me, doc = lax.axis_index("term"), lax.axis_index("doc")
    my_x, my_z = doc // 4, lax.rem(doc, 4)
    sums[...] = jnp.zeros_like(sums)
    h_all[0] = jnp.zeros((128, 128), jnp.bfloat16)
    for s in range(4):
        for b in range(4):
            same = lax.rem(me + 8 - 2 * s, 8)
            other = same + 1 - 2 * lax.rem(me, 2)
            h_all[1 + same * 4 + b] = near[s, b * 128 : (b + 1) * 128, :]
            h_all[1 + other * 4 + b] = far[s, b * 128 : (b + 1) * 128, :]
    plan_copy.wait()

    @pl.loop(0, pl.cdiv(plan[10 + half, 0], UNROLL))
    def _(step):
        found, targets = [], []
        for u in range(UNROLL):
            first = (step * UNROLL + u) * 4
            left, right = [], []
            for i in range(4):
                entry = plan[5 * half + first // 128, first % 128 + i]
                left.append(tiles[entry & 1023])
                right.append(h_all[(entry >> 10) & 63])
                if i == 0:
                    to_x, to_z = entry >> 18, (entry >> 16) & 3
                    if half == 0:
                        targets.append(((to_x + 4 - my_x) & 3) * 4 + to_z)
                    else:
                        targets.append(((to_z + 4 - my_z) & 3) * 4 + to_x)
            found.append(
                jnp.dot(
                    jnp.concatenate(left, axis=1),
                    jnp.concatenate(right, axis=0),
                    preferred_element_type=jnp.float32,
                )
            )
        for u in range(UNROLL):
            sums[targets[u]] += found[u]

    for s in range(4):
        for b in range(4):
            outs[s][b * 128 : b * 128 + 128] = sums[4 * s + b]
        outs[s][512:576] = gram[64 * half : 64 * half + 64]


def tile_products(half, plan, near, far, gram, tiles):
    return pl.pallas_call(
        functools.partial(products_kernel, half),
        out_shape=[jax.ShapeDtypeStruct((576, 128), jnp.float32)] * 4,
        in_specs=[pl.BlockSpec(memory_space=ANY)] + [pl.BlockSpec(memory_space=VMEM)] * 4,
        out_specs=[pl.BlockSpec(memory_space=VMEM)] * 4,
        scratch_shapes=[
            VMEM((16, 128, 128), jnp.float32),
            VMEM((33, 128, 128), jnp.bfloat16),
            SMEM((16, 128), jnp.int32),
            pltpu.SemaphoreType.DMA,
        ],
        cost_estimate=pl.CostEstimate(flops=4 * 10**9, bytes_accessed=10**7, transcendentals=0),
        compiler_params=pltpu.CompilerParams(vmem_limit_bytes=8 * 2**20),
    )(plan, near, far, gram, resident(tiles))


def regroup_kernel(half, *refs):
    pieces, outs = refs[:4], refs[-4:]
    doc = lax.axis_index("doc")
    mine = lax.rem(doc, 4) if half == 0 else doc // 4
    for s in range(4):
        first = pl.multiple_of(((mine + s) & 3) * 128, 128)
        part = pl.ds(first, 128)
        outs[s][0:128] = (pieces[0][part] + pieces[1][part]) + (pieces[2][part] + pieces[3][part])
    gram = (pieces[0][512:576] + pieces[1][512:576]) + (pieces[2][512:576] + pieces[3][512:576])
    for s in range(4):
        outs[s][128:192] = gram


def regroup(half, pieces, after=()):
    return pl.pallas_call(
        functools.partial(regroup_kernel, half),
        out_shape=[jax.ShapeDtypeStruct((192, 128), jnp.float32)] * 4,
        in_specs=[pl.BlockSpec(memory_space=VMEM)] * 4
        + [pl.BlockSpec(memory_space=ANY)] * len(after),
        out_specs=[pl.BlockSpec(memory_space=VMEM)] * 4,
        compiler_params=pltpu.CompilerParams(vmem_limit_bytes=8 * 2**20),
    )(*pieces, *after)


def sweep_kernel(*refs):
    first, second, (w, fresh, squares) = refs[:4], refs[4:8], refs[8:]
    upper = (first[0][...] + first[1][...]) + (first[2][...] + first[3][...])
    lower = (second[0][...] + second[1][...]) + (second[2][...] + second[3][...])
    cross_t = jnp.concatenate([upper[:128].T, lower[:128].T], axis=1)
    gram = jnp.concatenate([upper[128:], lower[128:]], axis=0)
    row_id = lax.broadcasted_iota(jnp.int32, (128, 128), 0)
    col_id = lax.broadcasted_iota(jnp.int32, (128, 128), 1)
    diagonal = jnp.sum(jnp.where(row_id == col_id, gram, 0.0), axis=1, keepdims=True)
    inverse = 1.0 / diagonal
    w_t = w[...].T
    rest = cross_t - jnp.dot(
        gram, w_t, precision=lax.Precision.HIGHEST, preferred_element_type=jnp.float32
    )
    estimate = w_t + rest * inverse
    scaled = jnp.where(col_id < row_id, gram * inverse, 0.0)
    groups = [estimate[8 * q : 8 * q + 8] for q in range(16)]
    for k in range(128):
        q, s = divmod(k, 8)
        change = jnp.maximum(groups[q][s : s + 1], 0.0) - w_t[k : k + 1]
        for later in range(q, 16):
            groups[later] = groups[later] - scaled[8 * later : 8 * later + 8, k : k + 1] * change
    updated = jnp.maximum(jnp.concatenate(groups, axis=0), 0.0).T
    fresh[...] = updated
    squares[...] = jnp.broadcast_to(
        jnp.sum(updated * updated, axis=0, keepdims=True), (128, 128)
    )


def sweep(first, second, w):
    return pl.pallas_call(
        sweep_kernel,
        out_shape=(
            jax.ShapeDtypeStruct((256, 128), jnp.float32),
            jax.ShapeDtypeStruct((128, 128), jnp.float32),
        ),
        in_specs=[pl.BlockSpec(memory_space=VMEM)] * 9,
        out_specs=[pl.BlockSpec(memory_space=VMEM)] * 2,
        compiler_params=pltpu.CompilerParams(vmem_limit_bytes=16 * 2**20),
    )(*first, *second, w)


def scale_kernel(total_rows, squares, updated, out):
    total = jnp.sum(squares[...], axis=0, keepdims=True)
    rms = jnp.sqrt(total / total_rows + 1e-06)
    out[...] = updated[...] / rms


def scale(squares, updated, total_rows):
    return pl.pallas_call(
        functools.partial(scale_kernel, total_rows),
        out_shape=jax.ShapeDtypeStruct(updated.shape, jnp.float32),
    )(resident(squares), resident(updated))


def body(doc_tiles, tile_rows, tile_cols, tile_count, factor_h, factor_w):
    tiles = doc_tiles[0]
    own = factor_h.T
    shifted = [along_y(own, s) for s in (1, 2, 3)]
    plan = make_plan(tile_rows, tile_cols, tile_count)
    near, plan = lax.optimization_barrier((jnp.stack([own] + shifted), plan))
    far = other_core(near)

    def self_gram(x):
        x = x.reshape(-1, 128)
        return lax.dot_general(x, x, (((0,), (0,)), ((), ())), preferred_element_type=jnp.float32)

    gram = self_gram(near) + self_gram(far)
    even = tile_products(0, plan, near, far, gram, tiles)
    odd = tile_products(1, plan, near, far, gram, tiles)
    after = odd[0]
    even = [even[0]] + [along_x(even[s], s) for s in (1, 2, 3)]
    odd = [odd[0]] + [along_z(odd[s], s) for s in (1, 2, 3)]
    even = regroup(0, even, [after])
    even = [even[0]] + [along_z(even[s], s) for s in (1, 2, 3)]
    odd = regroup(1, odd)
    odd = [odd[0]] + [along_x(odd[s], s) for s in (1, 2, 3)]
    updated, squares = sweep(even, odd, factor_w)
    shared = lax.all_to_all(squares.reshape(128, 1, 128), ("term", "doc"), 0, 0)
    return scale(shared.reshape(128, 128), updated, 32768)


def solution(mesh):
    in_specs = (
        P("term", "doc", None, None),
        P("term", "doc"),
        P("term", "doc"),
        P("term", "doc"),
        P(None, ("term", "doc")),
        P(("term", "doc"), None),
    )
    out_specs = P(("term", "doc"), None)
    return jax.shard_map(body, mesh=mesh, in_specs=in_specs, out_specs=out_specs, check_vma=False)
```

time: 106 us -> 82.8 us (0.78)
  blocking collectives: 55.7 us -> 21.4 us
  Pallas kernels: 24.5 us -> 8.75 us
  starting transfers between devices: 15.6 us -> 28.7 us
  waiting for transfers between devices: 5.14 us -> 13.9 us
  local copies, waits for them, and re-layouts: 2.84 us -> 8.15 us
    all_to_all x2 -> x1, blocking collectives: 55.7 us -> 21.4 us  [body(): shared = lax.all_to_all(squares.reshape(128, 1, 128), ('term', 'doc'), 0, 0)]
    ppermute x0 -> x12, starting transfers between devices: none -> 21.2 us  [the longest x6 12.6 us: along_z(): lax.ppermute(x, 'doc', [(i, i // 4 * 4 + (i + step) % 4) for i in range(1...]
    pallas_call x2 -> x6, Pallas kernels: 21.4 us -> 6.94 us  [the longest x2 5.23 us: tile_products(): pl.pallas_call(functools.partial(products_kernel, half), out_shape=[jax.S...]
    ppermute x0 -> x12, waiting for transfers between devices: none -> 11 us  [the longest x6 7.96 us: along_z(): lax.ppermute(x, 'doc', [(i, i // 4 * 4 + (i + step) % 4) for i in range(1...]
    all_to_all x1 -> x0, starting transfers between devices: 7.69 us -> none  [body(): grams = lax.all_to_all(jnp.broadcast_to(gram, (16, 128, 128)), 'doc', 0, 0)]
    unnamed x9, local copies, waits for them, and re-layouts: 1.68 us -> 8.15 us
    ppermute x3, waiting for transfers between devices: 3.6 us -> 1.76 us  [along_y(): return lax.ppermute(x, 'term', [(i, (i + 2 * step) % 8) for i in range(8)])]
    pallas_call x1, Pallas kernels: 3.02 us -> 1.82 us  [sweep(): pl.pallas_call(sweep_kernel, out_shape=(jax.ShapeDtypeStruct((256, 128),...]
  transfers between devices with their start and end apart: 5 -> 16, of which waited for: 3 -> 7; matrix products, arithmetic and copies ran while one was open for 0% -> 0% of each run, Pallas kernels for 19% -> 4%
where the time goes in v2:
time: 82.8 us; the launch traced here: 82.5 us
  starting transfers between devices  28.7 us (35%)
  blocking collectives  21.4 us (26%)
  waiting for transfers between devices  13.9 us (17%)
  Pallas kernels  8.75 us (11%)
  local copies, waits for them, and re-layouts  8.15 us (10%)
    all_to_all x1, blocking collectives, body(): shared = lax.all_to_all(squares.reshape(128, 1, 128), ('term', 'doc'), 0, 0)  21.4 us
    ppermute x6, starting transfers between devices, along_z(): lax.ppermute(x, 'doc', [(i, i // 4 * 4 + (i + step) % 4) for i in range(1...  12.6 us
    ppermute x6, starting transfers between devices, along_x(): return lax.ppermute(x, 'doc', [(i, (i + 4 * step) % 16) for i in range(16)])  8.63 us
    unnamed x9, local copies, waits for them, and re-layouts  8.15 us
    ppermute x6, waiting for transfers between devices, along_z(): lax.ppermute(x, 'doc', [(i, i // 4 * 4 + (i + step) % 4) for i in range(1...  7.96 us
    ppermute x3, starting transfers between devices, along_y(): return lax.ppermute(x, 'term', [(i, (i + 2 * step) % 8) for i in range(8)])  5.88 us
    pallas_call x2, Pallas kernels, tile_products(): pl.pallas_call(functools.partial(products_kernel, half), out_shape=[jax.S...  5.23 us
    ppermute x6, waiting for transfers between devices, along_x(): return lax.ppermute(x, 'doc', [(i, (i + 4 * step) % 16) for i in range(16)])  3.01 us
  transfers between devices with their start and end apart: 16, of which 7 were waited for; matrix products, arithmetic and copies ran while one was open for 0% of the time, Pallas kernels for 4%

profile of v2, /device:TPU:1, one launch (start us, length us, event | category | flops | bytes accessed | tf_op | source)
XLA Modules:
  0.0 82.5 jit_solution(9297861914989018998)
XLA Ops:
  0.0 1.0 %copy.10 = bf16[128,512]{0,1:T(8,128)(2,1)S(1)} copy(bf16[128,512]{1,0:T(8,128)(2,1)} %param.10) | data formatting | bytes 262144 | tf_op args[4]
  1.0 2.2 %collective-permute-start = (bf16[512,128]{1,0:T(8,128)(2,1)S(1)}, bf16[512,128]{1,0:T(8,128)(2,1)S(1)}, u32[]{:S(2)}, u32[]{:S(2)}) collective-permute-start(bf16[512,128]{1,0:T(8,128)(2,1)S(1)} %bitcast.25), channel_id=1, source_target_pairs={{0,32},{16,48},{32,64},{48,80},{64,96},{80,112},{96,0},{112,16},{1... | collective-permute-start | bytes 393224 | tf_op jit(solution)/shard_map/ppermute | solution.py:17
  3.2 2.6 %collective-permute-start.1 = (bf16[512,128]{1,0:T(8,128)(2,1)S(1)}, bf16[512,128]{1,0:T(8,128)(2,1)S(1)}, u32[]{:S(2)}, u32[]{:S(2)}) collective-permute-start(bf16[512,128]{1,0:T(8,128)(2,1)S(1)} %bitcast.26), channel_id=1, source_target_pairs={{0,64},{16,80},{32,96},{48,112},{64,0},{80,16},{96,32},{112,48},{1... | collective-permute-start | bytes 393224 | tf_op jit(solution)/shard_map/ppermute | solution.py:17
  5.8 1.1 %collective-permute-start.2 = (bf16[512,128]{1,0:T(8,128)(2,1)S(1)}, bf16[512,128]{1,0:T(8,128)(2,1)S(1)}, u32[]{:S(2)}, u32[]{:S(2)}) collective-permute-start(bf16[512,128]{1,0:T(8,128)(2,1)S(1)} %bitcast.27), channel_id=1, source_target_pairs={{0,96},{16,112},{32,0},{48,16},{64,32},{80,48},{96,64},{112,80},{1... | collective-permute-start | bytes 393224 | tf_op jit(solution)/shard_map/ppermute | solution.py:17
  9.8 1.8 %collective-permute-done.1 = bf16[512,128]{1,0:T(8,128)(2,1)S(1)} collective-permute-done((bf16[512,128]{1,0:T(8,128)(2,1)S(1)}, bf16[512,128]{1,0:T(8,128)(2,1)S(1)}, u32[]{:S(2)}, u32[]{:S(2)}) %collective-permute-start.1) | collective-permute-done | bytes 131104 | tf_op jit(solution)/shard_map/ppermute | solution.py:17
  11.6 1.6 %collective-permute-start.3 = (bf16[4,512,128]{2,1,0:T(8,128)(2,1)S(1)}, bf16[4,512,128]{2,1,0:T(8,128)(2,1)S(1)}, u32[]{:S(2)}, u32[]{:S(2)}) collective-permute-start(bf16[4,512,128]{2,1,0:T(8,128)(2,1)S(1)} %pad_maximum_fusion.near), channel_id=1, source_target_pairs={{0,16},{16,0},{32,48},{48,32},{64,80},{80,64},{96,112},{112,96},{1... | collective-permute-start | bytes 1572872 | tf_op jit(solution)/shard_map/ppermute | solution.py:21
  13.6 1.2 %collective-permute-done.3.far = bf16[4,512,128]{2,1,0:T(8,128)(2,1)S(1)} collective-permute-done((bf16[4,512,128]{2,1,0:T(8,128)(2,1)S(1)}, bf16[4,512,128]{2,1,0:T(8,128)(2,1)S(1)}, u32[]{:S(2)}, u32[]{:S(2)}) %collective-permute-start.3) | collective-permute-done | bytes 524320 | tf_op jit(solution)/shard_map/ppermute | solution.py:21
  15.1 5.8 %copy-done = bf16[1,512,128,128]{3,2,1,0:T(8,128)(2,1)S(1)} copy-done((bf16[1,512,128,128]{3,2,1,0:T(8,128)(2,1)S(1)}, bf16[1,512,128,128]{3,2,1,0:T(8,128)(2,1)}, u32[]{:S(2)}) %copy-start) | copy-done | bytes 16777240
  20.9 3.0 %shard_map.66 = (f32[576,128]{1,0:T(8,128)S(1)}, f32[576,128]{1,0:T(8,128)S(1)}, f32[576,128]{1,0:T(8,128)S(1)}, f32[576,128]{1,0:T(8,128)S(1)}) custom-call(s32[16,128]{1,0:T(8,128)S(1)} %shard_map.64.plan_in, bf16[4,512,128]{2,1,0:T(8,128)(2,1)S(1)} %pad_maximum_fusion.near, bf16[4,512,128]{2,1,0:T(8,128)(2,1)S(1)} %collective-permute-done.3.far, ...), custom_call_target="tpu_custom_call" | custom-call | flops 4000000000 | bytes 10000000 | tf_op jit(solution)/shard_map/pallas_call | solution.py:144
  23.9 2.4 %collective-permute-start.10 = (f32[576,128]{1,0:T(8,128)S(1)}, f32[576,128]{1,0:T(8,128)S(1)}, u32[]{:S(2)}, u32[]{:S(2)}) collective-permute-start(f32[576,128]{1,0:T(8,128)S(1)} %get-tuple-element.36), channel_id=1, source_target_pairs={{0,1},{1,2},{2,3},{3,0},{4,5},{5,6},{6,7},{7,4},{8,9},{9,10},{10,1... | collective-permute-start | bytes 884744 | tf_op jit(solution)/shard_map/ppermute | solution.py:29
  26.3 4.8 %collective-permute-start.11 = (f32[576,128]{1,0:T(8,128)S(1)}, f32[576,128]{1,0:T(8,128)S(1)}, u32[]{:S(2)}, u32[]{:S(2)}) collective-permute-start(f32[576,128]{1,0:T(8,128)S(1)} %get-tuple-element.37), channel_id=1, source_target_pairs={{0,2},{1,3},{2,0},{3,1},{4,6},{5,7},{6,4},{7,5},{8,10},{9,11},{10,... | collective-permute-start | bytes 884744 | tf_op jit(solution)/shard_map/ppermute | solution.py:29
  31.1 2.2 %shard_map.65 = (f32[576,128]{1,0:T(8,128)S(1)}, f32[576,128]{1,0:T(8,128)S(1)}, f32[576,128]{1,0:T(8,128)S(1)}, f32[576,128]{1,0:T(8,128)S(1)}) custom-call(s32[16,128]{1,0:T(8,128)S(1)} %shard_map.64.plan_in, bf16[4,512,128]{2,1,0:T(8,128)(2,1)S(1)} %pad_maximum_fusion.near, bf16[4,512,128]{2,1,0:T(8,128)(2,1)S(1)} %collective-permute-done.3.far, ...), custom_call_target="tpu_custom_call" | custom-call | flops 4000000000 | bytes 10000000 | tf_op jit(solution)/shard_map/pallas_call | solution.py:144
  33.4 2.7 %collective-permute-start.4 = (f32[576,128]{1,0:T(8,128)S(1)}, f32[576,128]{1,0:T(8,128)S(1)}, u32[]{:S(2)}, u32[]{:S(2)}) collective-permute-start(f32[576,128]{1,0:T(8,128)S(1)} %get-tuple-element.28), channel_id=1, source_target_pairs={{0,4},{1,5},{2,6},{3,7},{4,8},{5,9},{6,10},{7,11},{8,12},{9,13},{1... | collective-permute-start | bytes 884744 | tf_op jit(solution)/shard_map/ppermute | solution.py:25
  36.1 1.0 %collective-permute-start.5 = (f32[576,128]{1,0:T(8,128)S(1)}, f32[576,128]{1,0:T(8,128)S(1)}, u32[]{:S(2)}, u32[]{:S(2)}) collective-permute-start(f32[576,128]{1,0:T(8,128)S(1)} %get-tuple-element.29), channel_id=1, source_target_pairs={{0,8},{1,9},{2,10},{3,11},{4,12},{5,13},{6,14},{7,15},{8,0},{9,1},... | collective-permute-start | bytes 884744 | tf_op jit(solution)/shard_map/ppermute | solution.py:25
  37.1 1.8 %collective-permute-start.6 = (f32[576,128]{1,0:T(8,128)S(1)}, f32[576,128]{1,0:T(8,128)S(1)}, u32[]{:S(2)}, u32[]{:S(2)}) collective-permute-start(f32[576,128]{1,0:T(8,128)S(1)} %get-tuple-element.30), channel_id=1, source_target_pairs={{0,12},{1,13},{2,14},{3,15},{4,0},{5,1},{6,2},{7,3},{8,4},{9,5},{1... | collective-permute-start | bytes 884744 | tf_op jit(solution)/shard_map/ppermute | solution.py:25
  38.9 5.1 %collective-permute-done.11.refs_2_ = f32[576,128]{1,0:T(8,128)S(1)} collective-permute-done((f32[576,128]{1,0:T(8,128)S(1)}, f32[576,128]{1,0:T(8,128)S(1)}, u32[]{:S(2)}, u32[]{:S(2)}) %collective-permute-start.11) | collective-permute-done | bytes 294944 | tf_op jit(solution)/shard_map/ppermute | solution.py:29
  44.2 3.0 %collective-permute-start.14 = (f32[192,128]{1,0:T(8,128)S(1)}, f32[192,128]{1,0:T(8,128)S(1)}, u32[]{:S(2)}, u32[]{:S(2)}) collective-permute-start(f32[192,128]{1,0:T(8,128)S(1)} %get-tuple-element.41), channel_id=1, source_target_pairs={{0,8},{1,9},{2,10},{3,11},{4,12},{5,13},{6,14},{7,15},{8,0},{9,1},... | collective-permute-start | bytes 294920 | tf_op jit(solution)/shard_map/ppermute | solution.py:25
  47.3 2.0 %collective-permute-done.5.refs_2_ = f32[576,128]{1,0:T(8,128)S(1)} collective-permute-done((f32[576,128]{1,0:T(8,128)S(1)}, f32[576,128]{1,0:T(8,128)S(1)}, u32[]{:S(2)}, u32[]{:S(2)}) %collective-permute-start.5) | collective-permute-done | bytes 294944 | tf_op jit(solution)/shard_map/ppermute | solution.py:25
  49.4 3.2 %collective-permute-start.7 = (f32[192,128]{1,0:T(8,128)S(1)}, f32[192,128]{1,0:T(8,128)S(1)}, u32[]{:S(2)}, u32[]{:S(2)}) collective-permute-start(f32[192,128]{1,0:T(8,128)S(1)} %get-tuple-element.33), channel_id=1, source_target_pairs={{0,1},{1,2},{2,3},{3,0},{4,5},{5,6},{6,7},{7,4},{8,9},{9,10},{10,1... | collective-permute-start | bytes 294920 | tf_op jit(solution)/shard_map/ppermute | solution.py:29
  53.1 1.0 %collective-permute-done.13.refs_5_ = f32[192,128]{1,0:T(8,128)S(1)} collective-permute-done((f32[192,128]{1,0:T(8,128)S(1)}, f32[192,128]{1,0:T(8,128)S(1)}, u32[]{:S(2)}, u32[]{:S(2)}) %collective-permute-start.13) | collective-permute-done | bytes 98336 | tf_op jit(solution)/shard_map/ppermute | solution.py:25
  54.1 1.6 %collective-permute-start.9 = (f32[192,128]{1,0:T(8,128)S(1)}, f32[192,128]{1,0:T(8,128)S(1)}, u32[]{:S(2)}, u32[]{:S(2)}) collective-permute-start(f32[192,128]{1,0:T(8,128)S(1)} %get-tuple-element.35), channel_id=1, source_target_pairs={{0,3},{1,0},{2,1},{3,2},{4,7},{5,4},{6,5},{7,6},{8,11},{9,8},{10,9... | collective-permute-start | bytes 294920 | tf_op jit(solution)/shard_map/ppermute | solution.py:29
  55.7 2.6 %collective-permute-done.8.refs_2_ = f32[192,128]{1,0:T(8,128)S(1)} collective-permute-done((f32[192,128]{1,0:T(8,128)S(1)}, f32[192,128]{1,0:T(8,128)S(1)}, u32[]{:S(2)}, u32[]{:S(2)}) %collective-permute-start.8) | collective-permute-done | bytes 98336 | tf_op jit(solution)/shard_map/ppermute | solution.py:29
  58.5 1.8 %shard_map.69 = (f32[256,128]{1,0:T(8,128)S(1)}, f32[128,128]{1,0:T(8,128)S(1)}) custom-call(f32[192,128]{1,0:T(8,128)S(1)} %get-tuple-element.32.refs_0_, f32[192,128]{1,0:T(8,128)S(1)} %collective-permute-done.7.refs_1_, f32[192,128]{1,0:T(8,128)S(1)} %collective-permute-done.8.refs_2_, f32[192,128]{1,0:T(8,128)S(1)} %collective-permute-done.9.refs_3_, ...), custom_call_target="tpu_custom_call" | custom-call | tf_op jit(solution)/shard_map/pallas_call | solution.py:214
  60.4 21.4 %all_to_all.5 = f32[128,1,128]{2,1,0:T(1,128)S(1)} all-to-all(f32[128,1,128]{2,1,0:T(1,128)S(1)} %bitcast.24), channel_id=1, replica_groups=mesh['term'=8,'doc'=16] {'term','doc'}, dimensions={0} | all-to-all | bytes 131072 | tf_op jit(solution)/shard_map/all_to_all | solution.py:262
  (28 shorter events, 4.7 us)
Async XLA Ops:
  1.0 8.8 %collective-permute-start = (bf16[512,128]{1,0:T(8,128)(2,1)S(1)}, bf16[512,128]{1,0:T(8,128)(2,1)S(1)}, u32[]{:S(2)}, u32[]{:S(2)}) collective-permute-start(bf16[512,128]{1,0:T(8,128)(2,1)S(1)} %bitcast.25), channel_id=1, source_target_pairs={{0,32},{16,48},{32,64},{48,80},{64,96},{80,112},{96,0},{112,16},{1... | collective-permute-start | bytes 393224 | tf_op jit(solution)/shard_map/ppermute | solution.py:17
  3.2 8.3 %collective-permute-start.1 = (bf16[512,128]{1,0:T(8,128)(2,1)S(1)}, bf16[512,128]{1,0:T(8,128)(2,1)S(1)}, u32[]{:S(2)}, u32[]{:S(2)}) collective-permute-start(bf16[512,128]{1,0:T(8,128)(2,1)S(1)} %bitcast.26), channel_id=1, source_target_pairs={{0,64},{16,80},{32,96},{48,112},{64,0},{80,16},{96,32},{112,48},{1... | collective-permute-start | bytes 393224 | tf_op jit(solution)/shard_map/ppermute | solution.py:17
  5.8 5.7 %collective-permute-start.2 = (bf16[512,128]{1,0:T(8,128)(2,1)S(1)}, bf16[512,128]{1,0:T(8,128)(2,1)S(1)}, u32[]{:S(2)}, u32[]{:S(2)}) collective-permute-start(bf16[512,128]{1,0:T(8,128)(2,1)S(1)} %bitcast.27), channel_id=1, source_target_pairs={{0,96},{16,112},{32,0},{48,16},{64,32},{80,48},{96,64},{112,80},{1... | collective-permute-start | bytes 393224 | tf_op jit(solution)/shard_map/ppermute | solution.py:17
  7.6 0.7 copy-start.2
  8.2 0.7 copy-start.3
  11.6 3.2 %collective-permute-start.3 = (bf16[4,512,128]{2,1,0:T(8,128)(2,1)S(1)}, bf16[4,512,128]{2,1,0:T(8,128)(2,1)S(1)}, u32[]{:S(2)}, u32[]{:S(2)}) collective-permute-start(bf16[4,512,128]{2,1,0:T(8,128)(2,1)S(1)} %pad_maximum_fusion.near), channel_id=1, source_target_pairs={{0,16},{16,0},{32,48},{48,32},{64,80},{80,64},{96,112},{112,96},{1... | collective-permute-start | bytes 1572872 | tf_op jit(solution)/shard_map/ppermute | solution.py:21
  15.1 5.8 %copy-start = (bf16[1,512,128,128]{3,2,1,0:T(8,128)(2,1)S(1)}, bf16[1,512,128,128]{3,2,1,0:T(8,128)(2,1)}, u32[]{:S(2)}) copy-start(bf16[1,512,128,128]{3,2,1,0:T(8,128)(2,1)} %param.6) | copy-start | bytes 50331652
  20.9 37.6 %copy-start.1 = (f32[256,128]{1,0:T(8,128)S(1)}, f32[256,128]{1,0:T(8,128)}, u32[]{:S(2)}) copy-start(f32[256,128]{1,0:T(8,128)} %refs_8_.1) | copy-start | bytes 393220
  23.9 13.2 %collective-permute-start.10 = (f32[576,128]{1,0:T(8,128)S(1)}, f32[576,128]{1,0:T(8,128)S(1)}, u32[]{:S(2)}, u32[]{:S(2)}) collective-permute-start(f32[576,128]{1,0:T(8,128)S(1)} %get-tuple-element.36), channel_id=1, source_target_pairs={{0,1},{1,2},{2,3},{3,0},{4,5},{5,6},{6,7},{7,4},{8,9},{9,10},{10,1... | collective-permute-start | bytes 884744 | tf_op jit(solution)/shard_map/ppermute | solution.py:29
  26.3 17.7 %collective-permute-start.11 = (f32[576,128]{1,0:T(8,128)S(1)}, f32[576,128]{1,0:T(8,128)S(1)}, u32[]{:S(2)}, u32[]{:S(2)}) collective-permute-start(f32[576,128]{1,0:T(8,128)S(1)} %get-tuple-element.37), channel_id=1, source_target_pairs={{0,2},{1,3},{2,0},{3,1},{4,6},{5,7},{6,4},{7,5},{8,10},{9,11},{10,... | collective-permute-start | bytes 884744 | tf_op jit(solution)/shard_map/ppermute | solution.py:29
  31.1 12.9 %collective-permute-start.12 = (f32[576,128]{1,0:T(8,128)S(1)}, f32[576,128]{1,0:T(8,128)S(1)}, u32[]{:S(2)}, u32[]{:S(2)}) collective-permute-start(f32[576,128]{1,0:T(8,128)S(1)} %get-tuple-element.38), channel_id=1, source_target_pairs={{0,3},{1,0},{2,1},{3,2},{4,7},{5,4},{6,5},{7,6},{8,11},{9,8},{10,9... | collective-permute-start | bytes 884744 | tf_op jit(solution)/shard_map/ppermute | solution.py:29
  33.4 13.9 %collective-permute-start.4 = (f32[576,128]{1,0:T(8,128)S(1)}, f32[576,128]{1,0:T(8,128)S(1)}, u32[]{:S(2)}, u32[]{:S(2)}) collective-permute-start(f32[576,128]{1,0:T(8,128)S(1)} %get-tuple-element.28), channel_id=1, source_target_pairs={{0,4},{1,5},{2,6},{3,7},{4,8},{5,9},{6,10},{7,11},{8,12},{9,13},{1... | collective-permute-start | bytes 884744 | tf_op jit(solution)/shard_map/ppermute | solution.py:25
  36.1 13.2 %collective-permute-start.5 = (f32[576,128]{1,0:T(8,128)S(1)}, f32[576,128]{1,0:T(8,128)S(1)}, u32[]{:S(2)}, u32[]{:S(2)}) collective-permute-start(f32[576,128]{1,0:T(8,128)S(1)} %get-tuple-element.29), channel_id=1, source_target_pairs={{0,8},{1,9},{2,10},{3,11},{4,12},{5,13},{6,14},{7,15},{8,0},{9,1},... | collective-permute-start | bytes 884744 | tf_op jit(solution)/shard_map/ppermute | solution.py:25
  37.1 12.2 %collective-permute-start.6 = (f32[576,128]{1,0:T(8,128)S(1)}, f32[576,128]{1,0:T(8,128)S(1)}, u32[]{:S(2)}, u32[]{:S(2)}) collective-permute-start(f32[576,128]{1,0:T(8,128)S(1)} %get-tuple-element.30), channel_id=1, source_target_pairs={{0,12},{1,13},{2,14},{3,15},{4,0},{5,1},{6,2},{7,3},{8,4},{9,5},{1... | collective-permute-start | bytes 884744 | tf_op jit(solution)/shard_map/ppermute | solution.py:25
  44.2 9.9 %collective-permute-start.13 = (f32[192,128]{1,0:T(8,128)S(1)}, f32[192,128]{1,0:T(8,128)S(1)}, u32[]{:S(2)}, u32[]{:S(2)}) collective-permute-start(f32[192,128]{1,0:T(8,128)S(1)} %get-tuple-element.40), channel_id=1, source_target_pairs={{0,4},{1,5},{2,6},{3,7},{4,8},{5,9},{6,10},{7,11},{8,12},{9,13},{1... | collective-permute-start | bytes 294920 | tf_op jit(solution)/shard_map/ppermute | solution.py:25
  44.2 11.5 %collective-permute-start.14 = (f32[192,128]{1,0:T(8,128)S(1)}, f32[192,128]{1,0:T(8,128)S(1)}, u32[]{:S(2)}, u32[]{:S(2)}) collective-permute-start(f32[192,128]{1,0:T(8,128)S(1)} %get-tuple-element.41), channel_id=1, source_target_pairs={{0,8},{1,9},{2,10},{3,11},{4,12},{5,13},{6,14},{7,15},{8,0},{9,1},... | collective-permute-start | bytes 294920 | tf_op jit(solution)/shard_map/ppermute | solution.py:25
  47.3 8.5 %collective-permute-start.15 = (f32[192,128]{1,0:T(8,128)S(1)}, f32[192,128]{1,0:T(8,128)S(1)}, u32[]{:S(2)}, u32[]{:S(2)}) collective-permute-start(f32[192,128]{1,0:T(8,128)S(1)} %get-tuple-element.42), channel_id=1, source_target_pairs={{0,12},{1,13},{2,14},{3,15},{4,0},{5,1},{6,2},{7,3},{8,4},{9,5},{1... | collective-permute-start | bytes 294920 | tf_op jit(solution)/shard_map/ppermute | solution.py:25
  49.4 6.3 %collective-permute-start.7 = (f32[192,128]{1,0:T(8,128)S(1)}, f32[192,128]{1,0:T(8,128)S(1)}, u32[]{:S(2)}, u32[]{:S(2)}) collective-permute-start(f32[192,128]{1,0:T(8,128)S(1)} %get-tuple-element.33), channel_id=1, source_target_pairs={{0,1},{1,2},{2,3},{3,0},{4,5},{5,6},{6,7},{7,4},{8,9},{9,10},{10,1... | collective-permute-start | bytes 294920 | tf_op jit(solution)/shard_map/ppermute | solution.py:29
  52.6 5.7 %collective-permute-start.8 = (f32[192,128]{1,0:T(8,128)S(1)}, f32[192,128]{1,0:T(8,128)S(1)}, u32[]{:S(2)}, u32[]{:S(2)}) collective-permute-start(f32[192,128]{1,0:T(8,128)S(1)} %get-tuple-element.34), channel_id=1, source_target_pairs={{0,2},{1,3},{2,0},{3,1},{4,6},{5,7},{6,4},{7,5},{8,10},{9,11},{10,... | collective-permute-start | bytes 294920 | tf_op jit(solution)/shard_map/ppermute | solution.py:29
  54.1 4.4 %collective-permute-start.9 = (f32[192,128]{1,0:T(8,128)S(1)}, f32[192,128]{1,0:T(8,128)S(1)}, u32[]{:S(2)}, u32[]{:S(2)}) collective-permute-start(f32[192,128]{1,0:T(8,128)S(1)} %get-tuple-element.35), channel_id=1, source_target_pairs={{0,3},{1,0},{2,1},{3,2},{4,7},{5,4},{6,5},{7,6},{8,11},{9,8},{10,9... | collective-permute-start | bytes 294920 | tf_op jit(solution)/shard_map/ppermute | solution.py:29

commit v3 on v2

--- a/solution.py
+++ b/solution.py
@@ -7,7 +7,7 @@
 from jax.experimental.pallas import tpu as pltpu
 from jax.sharding import PartitionSpec as P
 
-UNROLL = 16
+UNROLL = 24
 ANY = pl.ANY
 VMEM = pltpu.VMEM
 SMEM = pltpu.SMEM
@@ -29,11 +29,21 @@
     return lax.ppermute(x, "doc", [(i, i // 4 * 4 + (i + step) % 4) for i in range(16)])
 
 
+def in_hbm(x):
+    return pltpu.with_memory_space_constraint(x, pltpu.HBM)
+
+
 def resident(x):
     return pltpu.with_memory_space_constraint(x, VMEM)
 
 
-def plan_kernel(rows, columns, count, plan):
+def plan_kernel(rows_in, columns_in, count, tiles, plan, rows, columns, sems):
+    rows_copy = pltpu.make_async_copy(rows_in, rows, sems.at[0])
+    columns_copy = pltpu.make_async_copy(columns_in, columns, sems.at[1])
+    rows_copy.start()
+    columns_copy.start()
+    rows_copy.wait()
+    columns_copy.wait()
     live = count[0, 0]
     c = columns[...]
     block = c // 64 * 4 + c % 4 + 1
@@ -81,15 +91,59 @@
     plan[12:16] = jnp.zeros((4, 128), jnp.int32)
 
 
-def make_plan(rows, columns, count):
+def make_plan(rows, columns, count, tiles):
     return pl.pallas_call(
         plan_kernel,
         out_shape=jax.ShapeDtypeStruct((16, 128), jnp.int32),
-        in_specs=[pl.BlockSpec(memory_space=VMEM)] * 2 + [pl.BlockSpec(memory_space=SMEM)],
+        in_specs=[pl.BlockSpec(memory_space=ANY)] * 2
+        + [pl.BlockSpec(memory_space=SMEM), pl.BlockSpec(memory_space=VMEM)],
         out_specs=pl.BlockSpec(memory_space=VMEM),
+        scratch_shapes=[
+            VMEM((1, 512), jnp.int32),
+            VMEM((1, 512), jnp.int32),
+            pltpu.SemaphoreType.DMA((2,)),
+        ],
         cost_estimate=pl.CostEstimate(flops=10**8, bytes_accessed=10**5, transcendentals=0),
         compiler_params=pltpu.CompilerParams(vmem_limit_bytes=8 * 2**20),
-    )(rows, columns, count)
+    )(in_hbm(rows), in_hbm(columns), count, resident(tiles))
+
+
+def partial_gram(shards):
+    total = None
+    for s in range(4):
+        x = shards[s]
+        part = lax.dot_general(x, x, (((0,), (0,)), ((), ())), preferred_element_type=jnp.float32)
+        total = part if total is None else total + part
+    return total
+
+
+def pack(shards):
+    return pl.pallas_call(
+        pack_only_kernel,
+        out_shape=jax.ShapeDtypeStruct((4, 512, 128), jnp.bfloat16),
+        in_specs=[pl.BlockSpec(memory_space=VMEM)] * 4,
+        out_specs=pl.BlockSpec(memory_space=VMEM),
+        compiler_params=pltpu.CompilerParams(vmem_limit_bytes=4 * 2**20),
+    )(*shards)
+
+
+def pack_only_kernel(own, first, second, third, near):
+    for s, shard in enumerate((own, first, second, third)):
+        near[s] = shard[...]
+
+
+def gram_kernel(shards, gram):
+    gram[...] = partial_gram(shards)
+
+
+def gram_of(shards):
+    return pl.pallas_call(
+        gram_kernel,
+        out_shape=jax.ShapeDtypeStruct((128, 128), jnp.float32),
+        in_specs=[pl.BlockSpec(memory_space=VMEM)],
+        out_specs=pl.BlockSpec(memory_space=VMEM),
+        compiler_params=pltpu.CompilerParams(vmem_limit_bytes=4 * 2**20),
+    )(shards)
 
 
 def products_kernel(half, plan_in, near, far, gram, tiles, *refs):
@@ -106,6 +160,8 @@
             other = same + 1 - 2 * lax.rem(me, 2)
             h_all[1 + same * 4 + b] = near[s, b * 128 : (b + 1) * 128, :]
             h_all[1 + other * 4 + b] = far[s, b * 128 : (b + 1) * 128, :]
+    if half == 0:
+        whole_gram = gram[...] + partial_gram(far)
     plan_copy.wait()
 
     @pl.loop(0, pl.cdiv(plan[10 + half, 0], UNROLL))
@@ -137,13 +193,14 @@
     for s in range(4):
         for b in range(4):
             outs[s][b * 128 : b * 128 + 128] = sums[4 * s + b]
-        outs[s][512:576] = gram[64 * half : 64 * half + 64]
+        if half == 0:
+            outs[s][512:640] = whole_gram
 
 
 def tile_products(half, plan, near, far, gram, tiles):
     return pl.pallas_call(
         functools.partial(products_kernel, half),
-        out_shape=[jax.ShapeDtypeStruct((576, 128), jnp.float32)] * 4,
+        out_shape=[jax.ShapeDtypeStruct((640 if half == 0 else 512, 128), jnp.float32)] * 4,
         in_specs=[pl.BlockSpec(memory_space=ANY)] + [pl.BlockSpec(memory_space=VMEM)] * 4,
         out_specs=[pl.BlockSpec(memory_space=VMEM)] * 4,
         scratch_shapes=[
@@ -152,7 +209,7 @@
             SMEM((16, 128), jnp.int32),
             pltpu.SemaphoreType.DMA,
         ],
-        cost_estimate=pl.CostEstimate(flops=4 * 10**9, bytes_accessed=10**7, transcendentals=0),
+        cost_estimate=pl.CostEstimate(flops=10**9, bytes_accessed=10**7, transcendentals=0),
         compiler_params=pltpu.CompilerParams(vmem_limit_bytes=8 * 2**20),
     )(plan, near, far, gram, resident(tiles))
 
@@ -165,15 +222,16 @@
         first = pl.multiple_of(((mine + s) & 3) * 128, 128)
         part = pl.ds(first, 128)
         outs[s][0:128] = (pieces[0][part] + pieces[1][part]) + (pieces[2][part] + pieces[3][part])
-    gram = (pieces[0][512:576] + pieces[1][512:576]) + (pieces[2][512:576] + pieces[3][512:576])
-    for s in range(4):
-        outs[s][128:192] = gram
+    if half == 0:
+        gram = (pieces[0][512:] + pieces[1][512:]) + (pieces[2][512:] + pieces[3][512:])
+        for s in range(4):
+            outs[s][128:256] = gram
 
 
 def regroup(half, pieces, after=()):
     return pl.pallas_call(
         functools.partial(regroup_kernel, half),
-        out_shape=[jax.ShapeDtypeStruct((192, 128), jnp.float32)] * 4,
+        out_shape=[jax.ShapeDtypeStruct((256 if half == 0 else 128, 128), jnp.float32)] * 4,
         in_specs=[pl.BlockSpec(memory_space=VMEM)] * 4
         + [pl.BlockSpec(memory_space=ANY)] * len(after),
         out_specs=[pl.BlockSpec(memory_space=VMEM)] * 4,
@@ -185,8 +243,8 @@
     first, second, (w, fresh, squares) = refs[:4], refs[4:8], refs[8:]
     upper = (first[0][...] + first[1][...]) + (first[2][...] + first[3][...])
     lower = (second[0][...] + second[1][...]) + (second[2][...] + second[3][...])
-    cross_t = jnp.concatenate([upper[:128].T, lower[:128].T], axis=1)
-    gram = jnp.concatenate([upper[128:], lower[128:]], axis=0)
+    cross_t = jnp.concatenate([upper[:128].T, lower.T], axis=1)
+    gram = upper[128:]
     row_id = lax.broadcasted_iota(jnp.int32, (128, 128), 0)
     col_id = lax.broadcasted_iota(jnp.int32, (128, 128), 1)
     diagonal = jnp.sum(jnp.where(row_id == col_id, gram, 0.0), axis=1, keepdims=True)
@@ -240,15 +298,11 @@
     tiles = doc_tiles[0]
     own = factor_h.T
     shifted = [along_y(own, s) for s in (1, 2, 3)]
-    plan = make_plan(tile_rows, tile_cols, tile_count)
-    near, plan = lax.optimization_barrier((jnp.stack([own] + shifted), plan))
+    plan = make_plan(tile_rows, tile_cols, tile_count, tiles)
+    near, plan = lax.optimization_barrier((pack([own] + shifted), plan))
     far = other_core(near)
 
-    def self_gram(x):
-        x = x.reshape(-1, 128)
-        return lax.dot_general(x, x, (((0,), (0,)), ((), ())), preferred_element_type=jnp.float32)
-
-    gram = self_gram(near) + self_gram(far)
+    gram = gram_of(near)
     even = tile_products(0, plan, near, far, gram, tiles)
     odd = tile_products(1, plan, near, far, gram, tiles)
     after = odd[0]

time: 82.8 us -> 76.7 us (0.926)
  blocking collectives: 21.4 us -> 16.9 us
  starting transfers between devices: 28.7 us -> 25.6 us
  Pallas kernels: 8.75 us -> 11.2 us
  waiting for transfers between devices: 13.9 us -> 15.5 us
  local copies, waits for them, and re-layouts: 8.15 us -> 6.79 us
    all_to_all x1, blocking collectives: 21.4 us -> 16.9 us  [body(): shared = lax.all_to_all(squares.reshape(128, 1, 128), ('term', 'doc'), 0, 0)]
    ppermute x6, waiting for transfers between devices: 7.96 us -> 11.7 us  [along_z(): lax.ppermute(x, 'doc', [(i, i // 4 * 4 + (i + step) % 4) for i in range(1...]
    ppermute x6, starting transfers between devices: 12.6 us -> 9.8 us  [along_z(): lax.ppermute(x, 'doc', [(i, i // 4 * 4 + (i + step) % 4) for i in range(1...]
    ppermute x3, waiting for transfers between devices: 1.76 us -> 0.01 us  [along_y(): return lax.ppermute(x, 'term', [(i, (i + 2 * step) % 8) for i in range(8)])]
    pallas_call x2, Pallas kernels: 5.23 us -> 6.6 us  [tile_products(): pl.pallas_call(functools.partial(products_kernel, half), out_shape=[jax.S...]
    unnamed x9 -> x5, local copies, waits for them, and re-layouts: 8.15 us -> 6.79 us
  transfers between devices with their start and end apart: 16 -> 16, of which waited for: 7 -> 5; matrix products, arithmetic and copies ran while one was open for 0% -> 0% of each run, Pallas kernels for 4% -> 6%
where the time goes in v3:
time: 76.7 us; the launch traced here: 76.8 us
  starting transfers between devices  25.6 us (33%)
  blocking collectives  16.9 us (22%)
  waiting for transfers between devices  15.5 us (20%)
  Pallas kernels  11.2 us (15%)
  local copies, waits for them, and re-layouts  6.79 us (9%)
  between operations  0.8 us (1%)
    all_to_all x1, blocking collectives, body(): shared = lax.all_to_all(squares.reshape(128, 1, 128), ('term', 'doc'), 0, 0)  16.9 us
    ppermute x6, waiting for transfers between devices, along_z(): lax.ppermute(x, 'doc', [(i, i // 4 * 4 + (i + step) % 4) for i in range(1...  11.7 us
    ppermute x6, starting transfers between devices, along_z(): lax.ppermute(x, 'doc', [(i, i // 4 * 4 + (i + step) % 4) for i in range(1...  9.8 us
    ppermute x6, starting transfers between devices, along_x(): return lax.ppermute(x, 'doc', [(i, (i + 4 * step) % 16) for i in range(16)])  8.3 us
    unnamed x5, local copies, waits for them, and re-layouts  6.79 us
    pallas_call x2, Pallas kernels, tile_products(): pl.pallas_call(functools.partial(products_kernel, half), out_shape=[jax.S...  6.6 us
    ppermute x3, starting transfers between devices, along_y(): return lax.ppermute(x, 'term', [(i, (i + 2 * step) % 8) for i in range(8)])  5.88 us
    ppermute x6, waiting for transfers between devices, along_x(): return lax.ppermute(x, 'doc', [(i, (i + 4 * step) % 16) for i in range(16)])  2.69 us
  transfers between devices with their start and end apart: 16, of which 5 were waited for; matrix products, arithmetic and copies ran while one was open for 0% of the time, Pallas kernels for 6%

profile of v3, /device:TPU:1, one launch (start us, length us, event | category | flops | bytes accessed | tf_op | source)
XLA Modules:
  0.0 76.8 jit_solution(3021874658737358062)
XLA Ops:
  0.0 1.0 %copy.8 = bf16[128,512]{0,1:T(8,128)(2,1)S(1)} copy(bf16[128,512]{1,0:T(8,128)(2,1)} %param.10) | data formatting | bytes 262144 | tf_op args[4]
  1.0 2.2 %collective-permute-start = (bf16[512,128]{1,0:T(8,128)(2,1)S(1)}, bf16[512,128]{1,0:T(8,128)(2,1)S(1)}, u32[]{:S(2)}, u32[]{:S(2)}) collective-permute-start(bf16[512,128]{1,0:T(8,128)(2,1)S(1)} %bitcast.9), channel_id=1, source_target_pairs={{0,32},{16,48},{32,64},{48,80},{64,96},{80,112},{96,0},{112,16},{1... | collective-permute-start | bytes 393224 | tf_op jit(solution)/shard_map/ppermute | solution.py:17
  3.2 2.6 %collective-permute-start.1 = (bf16[512,128]{1,0:T(8,128)(2,1)S(1)}, bf16[512,128]{1,0:T(8,128)(2,1)S(1)}, u32[]{:S(2)}, u32[]{:S(2)}) collective-permute-start(bf16[512,128]{1,0:T(8,128)(2,1)S(1)} %bitcast.10), channel_id=1, source_target_pairs={{0,64},{16,80},{32,96},{48,112},{64,0},{80,16},{96,32},{112,48},{1... | collective-permute-start | bytes 393224 | tf_op jit(solution)/shard_map/ppermute | solution.py:17
  5.8 1.1 %collective-permute-start.2 = (bf16[512,128]{1,0:T(8,128)(2,1)S(1)}, bf16[512,128]{1,0:T(8,128)(2,1)S(1)}, u32[]{:S(2)}, u32[]{:S(2)}) collective-permute-start(bf16[512,128]{1,0:T(8,128)(2,1)S(1)} %bitcast.11), channel_id=1, source_target_pairs={{0,96},{16,112},{32,0},{48,16},{64,32},{80,48},{96,64},{112,80},{1... | collective-permute-start | bytes 393224 | tf_op jit(solution)/shard_map/ppermute | solution.py:17
  7.6 5.8 %copy-done = bf16[1,512,128,128]{3,2,1,0:T(8,128)(2,1)S(1)} copy-done((bf16[1,512,128,128]{3,2,1,0:T(8,128)(2,1)S(1)}, bf16[1,512,128,128]{3,2,1,0:T(8,128)(2,1)}, u32[]{:S(2)}) %copy-start) | copy-done | bytes 16777240
  13.3 1.5 %shard_map.65.plan_in = s32[16,128]{1,0:T(8,128)S(1)} custom-call(s32[1,512]{1,0:T(1,128)} %rows_in.1, s32[1,512]{1,0:T(1,128)} %columns_in.1, s32[1,1]{1,0:T(1,128)S(6)} %copy.10.count, bf16[512,128,128]{2,1,0:T(8,128)(2,1)S(1)} %bitcast.6), custom_call_target="tpu_custom_call" | custom-call | flops 100000000 | bytes 100000 | tf_op jit(solution)/shard_map/pallas_call | solution.py:95
  15.0 1.6 %collective-permute-start.3 = (bf16[4,512,128]{2,1,0:T(8,128)(2,1)S(1)}, bf16[4,512,128]{2,1,0:T(8,128)(2,1)S(1)}, u32[]{:S(2)}, u32[]{:S(2)}) collective-permute-start(bf16[4,512,128]{2,1,0:T(8,128)(2,1)S(1)} %shard_map.64.shards.near), channel_id=1, source_target_pairs={{0,16},{16,0},{32,48},{48,32},{64,80},{80,64},{96,112},{112,96},{1... | collective-permute-start | bytes 1572872 | tf_op jit(solution)/shard_map/ppermute | solution.py:21
  16.9 1.2 %collective-permute-done.3.far = bf16[4,512,128]{2,1,0:T(8,128)(2,1)S(1)} collective-permute-done((bf16[4,512,128]{2,1,0:T(8,128)(2,1)S(1)}, bf16[4,512,128]{2,1,0:T(8,128)(2,1)S(1)}, u32[]{:S(2)}, u32[]{:S(2)}) %collective-permute-start.3) | collective-permute-done | bytes 524320 | tf_op jit(solution)/shard_map/ppermute | solution.py:21
  18.1 3.8 %shard_map.68 = (f32[512,128]{1,0:T(8,128)S(1)}, f32[512,128]{1,0:T(8,128)S(1)}, f32[512,128]{1,0:T(8,128)S(1)}, f32[512,128]{1,0:T(8,128)S(1)}) custom-call(s32[16,128]{1,0:T(8,128)S(1)} %shard_map.65.plan_in, bf16[4,512,128]{2,1,0:T(8,128)(2,1)S(1)} %shard_map.64.shards.near, bf16[4,512,128]{2,1,0:T(8,128)(2,1)S(1)} %collective-permute-done.3.far, ...), custom_call_target="tpu_custom_call" | custom-call | flops 1000000000 | bytes 10000000 | tf_op jit(solution)/shard_map/pallas_call | solution.py:201
  21.9 1.7 %collective-permute-start.10 = (f32[512,128]{1,0:T(8,128)S(1)}, f32[512,128]{1,0:T(8,128)S(1)}, u32[]{:S(2)}, u32[]{:S(2)}) collective-permute-start(f32[512,128]{1,0:T(8,128)S(1)} %get-tuple-element.36), channel_id=1, source_target_pairs={{0,1},{1,2},{2,3},{3,0},{4,5},{5,6},{6,7},{7,4},{8,9},{9,10},{10,1... | collective-permute-start | bytes 786440 | tf_op jit(solution)/shard_map/ppermute | solution.py:29
  23.6 2.8 %shard_map.67 = (f32[640,128]{1,0:T(8,128)S(1)}, f32[640,128]{1,0:T(8,128)S(1)}, f32[640,128]{1,0:T(8,128)S(1)}, f32[640,128]{1,0:T(8,128)S(1)}) custom-call(s32[16,128]{1,0:T(8,128)S(1)} %shard_map.65.plan_in, bf16[4,512,128]{2,1,0:T(8,128)(2,1)S(1)} %shard_map.64.shards.near, bf16[4,512,128]{2,1,0:T(8,128)(2,1)S(1)} %collective-permute-done.3.far, ...), custom_call_target="tpu_custom_call" | custom-call | flops 1000000000 | bytes 10000000 | tf_op jit(solution)/shard_map/pallas_call | solution.py:201
  26.4 1.3 %collective-permute-start.4 = (f32[640,128]{1,0:T(8,128)S(1)}, f32[640,128]{1,0:T(8,128)S(1)}, u32[]{:S(2)}, u32[]{:S(2)}) collective-permute-start(f32[640,128]{1,0:T(8,128)S(1)} %get-tuple-element.28), channel_id=1, source_target_pairs={{0,4},{1,5},{2,6},{3,7},{4,8},{5,9},{6,10},{7,11},{8,12},{9,13},{1... | collective-permute-start | bytes 983048 | tf_op jit(solution)/shard_map/ppermute | solution.py:25
  27.7 1.6 %collective-permute-start.5 = (f32[640,128]{1,0:T(8,128)S(1)}, f32[640,128]{1,0:T(8,128)S(1)}, u32[]{:S(2)}, u32[]{:S(2)}) collective-permute-start(f32[640,128]{1,0:T(8,128)S(1)} %get-tuple-element.29), channel_id=1, source_target_pairs={{0,8},{1,9},{2,10},{3,11},{4,12},{5,13},{6,14},{7,15},{8,0},{9,1},... | collective-permute-start | bytes 983048 | tf_op jit(solution)/shard_map/ppermute | solution.py:25
  29.3 2.0 %collective-permute-start.6 = (f32[640,128]{1,0:T(8,128)S(1)}, f32[640,128]{1,0:T(8,128)S(1)}, u32[]{:S(2)}, u32[]{:S(2)}) collective-permute-start(f32[640,128]{1,0:T(8,128)S(1)} %get-tuple-element.30), channel_id=1, source_target_pairs={{0,12},{1,13},{2,14},{3,15},{4,0},{5,1},{6,2},{7,3},{8,4},{9,5},{1... | collective-permute-start | bytes 983048 | tf_op jit(solution)/shard_map/ppermute | solution.py:25
  31.3 4.3 %collective-permute-start.11 = (f32[512,128]{1,0:T(8,128)S(1)}, f32[512,128]{1,0:T(8,128)S(1)}, u32[]{:S(2)}, u32[]{:S(2)}) collective-permute-start(f32[512,128]{1,0:T(8,128)S(1)} %get-tuple-element.37), channel_id=1, source_target_pairs={{0,2},{1,3},{2,0},{3,1},{4,6},{5,7},{6,4},{7,5},{8,10},{9,11},{10,... | collective-permute-start | bytes 786440 | tf_op jit(solution)/shard_map/ppermute | solution.py:29
  35.6 6.6 %collective-permute-done.11.refs_2_ = f32[512,128]{1,0:T(8,128)S(1)} collective-permute-done((f32[512,128]{1,0:T(8,128)S(1)}, f32[512,128]{1,0:T(8,128)S(1)}, u32[]{:S(2)}, u32[]{:S(2)}) %collective-permute-start.11) | collective-permute-done | bytes 262176 | tf_op jit(solution)/shard_map/ppermute | solution.py:29
  42.3 5.0 %collective-permute-done.12.refs_3_ = f32[512,128]{1,0:T(8,128)S(1)} collective-permute-done((f32[512,128]{1,0:T(8,128)S(1)}, f32[512,128]{1,0:T(8,128)S(1)}, u32[]{:S(2)}, u32[]{:S(2)}) %collective-permute-start.12) | collective-permute-done | bytes 262176 | tf_op jit(solution)/shard_map/ppermute | solution.py:29
  47.5 1.1 %collective-permute-start.7 = (f32[256,128]{1,0:T(8,128)S(1)}, f32[256,128]{1,0:T(8,128)S(1)}, u32[]{:S(2)}, u32[]{:S(2)}) collective-permute-start(f32[256,128]{1,0:T(8,128)S(1)} %get-tuple-element.33), channel_id=1, source_target_pairs={{0,1},{1,2},{2,3},{3,0},{4,5},{5,6},{6,7},{7,4},{8,9},{9,10},{10,1... | collective-permute-start | bytes 393224 | tf_op jit(solution)/shard_map/ppermute | solution.py:29
  48.7 2.6 %collective-permute-start.8 = (f32[256,128]{1,0:T(8,128)S(1)}, f32[256,128]{1,0:T(8,128)S(1)}, u32[]{:S(2)}, u32[]{:S(2)}) collective-permute-start(f32[256,128]{1,0:T(8,128)S(1)} %get-tuple-element.34), channel_id=1, source_target_pairs={{0,2},{1,3},{2,0},{3,1},{4,6},{5,7},{6,4},{7,5},{8,10},{9,11},{10,... | collective-permute-start | bytes 393224 | tf_op jit(solution)/shard_map/ppermute | solution.py:29
  51.3 2.6 %collective-permute-start.14 = (f32[128,128]{1,0:T(8,128)S(1)}, f32[128,128]{1,0:T(8,128)S(1)}, u32[]{:S(2)}, u32[]{:S(2)}) collective-permute-start(f32[128,128]{1,0:T(8,128)S(1)} %get-tuple-element.41), channel_id=1, source_target_pairs={{0,8},{1,9},{2,10},{3,11},{4,12},{5,13},{6,14},{7,15},{8,0},{9,1},... | collective-permute-start | bytes 196616 | tf_op jit(solution)/shard_map/ppermute | solution.py:25
  54.7 1.3 %collective-permute-done.14.refs_6_ = f32[128,128]{1,0:T(8,128)S(1)} collective-permute-done((f32[128,128]{1,0:T(8,128)S(1)}, f32[128,128]{1,0:T(8,128)S(1)}, u32[]{:S(2)}, u32[]{:S(2)}) %collective-permute-start.14) | collective-permute-done | bytes 65568 | tf_op jit(solution)/shard_map/ppermute | solution.py:25
  55.9 1.4 %collective-permute-done.15.refs_7_ = f32[128,128]{1,0:T(8,128)S(1)} collective-permute-done((f32[128,128]{1,0:T(8,128)S(1)}, f32[128,128]{1,0:T(8,128)S(1)}, u32[]{:S(2)}, u32[]{:S(2)}) %collective-permute-start.15) | collective-permute-done | bytes 65568 | tf_op jit(solution)/shard_map/ppermute | solution.py:25
  57.4 1.8 %shard_map.71 = (f32[256,128]{1,0:T(8,128)S(1)}, f32[128,128]{1,0:T(8,128)S(1)}) custom-call(f32[256,128]{1,0:T(8,128)S(1)} %get-tuple-element.32.refs_0_, f32[256,128]{1,0:T(8,128)S(1)} %collective-permute-done.7.refs_1_, f32[256,128]{1,0:T(8,128)S(1)} %collective-permute-done.8.refs_2_, f32[256,128]{1,0:T(8,128)S(1)} %collective-permute-done.9.refs_3_, ...), custom_call_target="tpu_custom_call" | custom-call | tf_op jit(solution)/shard_map/pallas_call | solution.py:272
  59.2 16.9 %all_to_all.5 = f32[128,1,128]{2,1,0:T(1,128)S(1)} all-to-all(f32[128,1,128]{2,1,0:T(1,128)S(1)} %bitcast.14), channel_id=1, replica_groups=mesh['term'=8,'doc'=16] {'term','doc'}, dimensions={0} | all-to-all | bytes 131072 | tf_op jit(solution)/shard_map/all_to_all | solution.py:316
  (23 shorter events, 2.1 us)
Async XLA Ops:
  1.0 13.9 %collective-permute-start = (bf16[512,128]{1,0:T(8,128)(2,1)S(1)}, bf16[512,128]{1,0:T(8,128)(2,1)S(1)}, u32[]{:S(2)}, u32[]{:S(2)}) collective-permute-start(bf16[512,128]{1,0:T(8,128)(2,1)S(1)} %bitcast.9), channel_id=1, source_target_pairs={{0,32},{16,48},{32,64},{48,80},{64,96},{80,112},{96,0},{112,16},{1... | collective-permute-start | bytes 393224 | tf_op jit(solution)/shard_map/ppermute | solution.py:17
  3.2 11.7 %collective-permute-start.1 = (bf16[512,128]{1,0:T(8,128)(2,1)S(1)}, bf16[512,128]{1,0:T(8,128)(2,1)S(1)}, u32[]{:S(2)}, u32[]{:S(2)}) collective-permute-start(bf16[512,128]{1,0:T(8,128)(2,1)S(1)} %bitcast.10), channel_id=1, source_target_pairs={{0,64},{16,80},{32,96},{48,112},{64,0},{80,16},{96,32},{112,48},{1... | collective-permute-start | bytes 393224 | tf_op jit(solution)/shard_map/ppermute | solution.py:17
  5.8 9.1 %collective-permute-start.2 = (bf16[512,128]{1,0:T(8,128)(2,1)S(1)}, bf16[512,128]{1,0:T(8,128)(2,1)S(1)}, u32[]{:S(2)}, u32[]{:S(2)}) collective-permute-start(bf16[512,128]{1,0:T(8,128)(2,1)S(1)} %bitcast.11), channel_id=1, source_target_pairs={{0,96},{16,112},{32,0},{48,16},{64,32},{80,48},{96,64},{112,80},{1... | collective-permute-start | bytes 393224 | tf_op jit(solution)/shard_map/ppermute | solution.py:17
  7.6 5.8 %copy-start = (bf16[1,512,128,128]{3,2,1,0:T(8,128)(2,1)S(1)}, bf16[1,512,128,128]{3,2,1,0:T(8,128)(2,1)}, u32[]{:S(2)}) copy-start(bf16[1,512,128,128]{3,2,1,0:T(8,128)(2,1)} %param.6) | copy-start | bytes 50331652
  15.0 3.1 %collective-permute-start.3 = (bf16[4,512,128]{2,1,0:T(8,128)(2,1)S(1)}, bf16[4,512,128]{2,1,0:T(8,128)(2,1)S(1)}, u32[]{:S(2)}, u32[]{:S(2)}) collective-permute-start(bf16[4,512,128]{2,1,0:T(8,128)(2,1)S(1)} %shard_map.64.shards.near), channel_id=1, source_target_pairs={{0,16},{16,0},{32,48},{48,32},{64,80},{80,64},{96,112},{112,96},{1... | collective-permute-start | bytes 1572872 | tf_op jit(solution)/shard_map/ppermute | solution.py:21
  16.9 40.5 %copy-start.1 = (f32[256,128]{1,0:T(8,128)S(1)}, f32[256,128]{1,0:T(8,128)}, u32[]{:S(2)}) copy-start(f32[256,128]{1,0:T(8,128)} %refs_8_.1) | copy-start | bytes 393220
  21.9 13.7 %collective-permute-start.10 = (f32[512,128]{1,0:T(8,128)S(1)}, f32[512,128]{1,0:T(8,128)S(1)}, u32[]{:S(2)}, u32[]{:S(2)}) collective-permute-start(f32[512,128]{1,0:T(8,128)S(1)} %get-tuple-element.36), channel_id=1, source_target_pairs={{0,1},{1,2},{2,3},{3,0},{4,5},{5,6},{6,7},{7,4},{8,9},{9,10},{10,1... | collective-permute-start | bytes 786440 | tf_op jit(solution)/shard_map/ppermute | solution.py:29
  26.4 21.0 %collective-permute-start.4 = (f32[640,128]{1,0:T(8,128)S(1)}, f32[640,128]{1,0:T(8,128)S(1)}, u32[]{:S(2)}, u32[]{:S(2)}) collective-permute-start(f32[640,128]{1,0:T(8,128)S(1)} %get-tuple-element.28), channel_id=1, source_target_pairs={{0,4},{1,5},{2,6},{3,7},{4,8},{5,9},{6,10},{7,11},{8,12},{9,13},{1... | collective-permute-start | bytes 983048 | tf_op jit(solution)/shard_map/ppermute | solution.py:25
  27.7 19.7 %collective-permute-start.5 = (f32[640,128]{1,0:T(8,128)S(1)}, f32[640,128]{1,0:T(8,128)S(1)}, u32[]{:S(2)}, u32[]{:S(2)}) collective-permute-start(f32[640,128]{1,0:T(8,128)S(1)} %get-tuple-element.29), channel_id=1, source_target_pairs={{0,8},{1,9},{2,10},{3,11},{4,12},{5,13},{6,14},{7,15},{8,0},{9,1},... | collective-permute-start | bytes 983048 | tf_op jit(solution)/shard_map/ppermute | solution.py:25
  29.3 18.1 %collective-permute-start.6 = (f32[640,128]{1,0:T(8,128)S(1)}, f32[640,128]{1,0:T(8,128)S(1)}, u32[]{:S(2)}, u32[]{:S(2)}) collective-permute-start(f32[640,128]{1,0:T(8,128)S(1)} %get-tuple-element.30), channel_id=1, source_target_pairs={{0,12},{1,13},{2,14},{3,15},{4,0},{5,1},{6,2},{7,3},{8,4},{9,5},{1... | collective-permute-start | bytes 983048 | tf_op jit(solution)/shard_map/ppermute | solution.py:25
  31.3 10.9 %collective-permute-start.11 = (f32[512,128]{1,0:T(8,128)S(1)}, f32[512,128]{1,0:T(8,128)S(1)}, u32[]{:S(2)}, u32[]{:S(2)}) collective-permute-start(f32[512,128]{1,0:T(8,128)S(1)} %get-tuple-element.37), channel_id=1, source_target_pairs={{0,2},{1,3},{2,0},{3,1},{4,6},{5,7},{6,4},{7,5},{8,10},{9,11},{10,... | collective-permute-start | bytes 786440 | tf_op jit(solution)/shard_map/ppermute | solution.py:29
  35.6 11.7 %collective-permute-start.12 = (f32[512,128]{1,0:T(8,128)S(1)}, f32[512,128]{1,0:T(8,128)S(1)}, u32[]{:S(2)}, u32[]{:S(2)}) collective-permute-start(f32[512,128]{1,0:T(8,128)S(1)} %get-tuple-element.38), channel_id=1, source_target_pairs={{0,3},{1,0},{2,1},{3,2},{4,7},{5,4},{6,5},{7,6},{8,11},{9,8},{10,9... | collective-permute-start | bytes 786440 | tf_op jit(solution)/shard_map/ppermute | solution.py:29
  47.3 6.6 %collective-permute-start.13 = (f32[128,128]{1,0:T(8,128)S(1)}, f32[128,128]{1,0:T(8,128)S(1)}, u32[]{:S(2)}, u32[]{:S(2)}) collective-permute-start(f32[128,128]{1,0:T(8,128)S(1)} %get-tuple-element.40), channel_id=1, source_target_pairs={{0,4},{1,5},{2,6},{3,7},{4,8},{5,9},{6,10},{7,11},{8,12},{9,13},{1... | collective-permute-start | bytes 196616 | tf_op jit(solution)/shard_map/ppermute | solution.py:25
  47.5 9.8 %collective-permute-start.7 = (f32[256,128]{1,0:T(8,128)S(1)}, f32[256,128]{1,0:T(8,128)S(1)}, u32[]{:S(2)}, u32[]{:S(2)}) collective-permute-start(f32[256,128]{1,0:T(8,128)S(1)} %get-tuple-element.33), channel_id=1, source_target_pairs={{0,1},{1,2},{2,3},{3,0},{4,5},{5,6},{6,7},{7,4},{8,9},{9,10},{10,1... | collective-permute-start | bytes 393224 | tf_op jit(solution)/shard_map/ppermute | solution.py:29
  48.7 8.7 %collective-permute-start.8 = (f32[256,128]{1,0:T(8,128)S(1)}, f32[256,128]{1,0:T(8,128)S(1)}, u32[]{:S(2)}, u32[]{:S(2)}) collective-permute-start(f32[256,128]{1,0:T(8,128)S(1)} %get-tuple-element.34), channel_id=1, source_target_pairs={{0,2},{1,3},{2,0},{3,1},{4,6},{5,7},{6,4},{7,5},{8,10},{9,11},{10,... | collective-permute-start | bytes 393224 | tf_op jit(solution)/shard_map/ppermute | solution.py:29
  51.3 6.0 %collective-permute-start.9 = (f32[256,128]{1,0:T(8,128)S(1)}, f32[256,128]{1,0:T(8,128)S(1)}, u32[]{:S(2)}, u32[]{:S(2)}) collective-permute-start(f32[256,128]{1,0:T(8,128)S(1)} %get-tuple-element.35), channel_id=1, source_target_pairs={{0,3},{1,0},{2,1},{3,2},{4,7},{5,4},{6,5},{7,6},{8,11},{9,8},{10,9... | collective-permute-start | bytes 393224 | tf_op jit(solution)/shard_map/ppermute | solution.py:29
  51.3 4.6 %collective-permute-start.14 = (f32[128,128]{1,0:T(8,128)S(1)}, f32[128,128]{1,0:T(8,128)S(1)}, u32[]{:S(2)}, u32[]{:S(2)}) collective-permute-start(f32[128,128]{1,0:T(8,128)S(1)} %get-tuple-element.41), channel_id=1, source_target_pairs={{0,8},{1,9},{2,10},{3,11},{4,12},{5,13},{6,14},{7,15},{8,0},{9,1},... | collective-permute-start | bytes 196616 | tf_op jit(solution)/shard_map/ppermute | solution.py:25
  53.9 3.4 %collective-permute-start.15 = (f32[128,128]{1,0:T(8,128)S(1)}, f32[128,128]{1,0:T(8,128)S(1)}, u32[]{:S(2)}, u32[]{:S(2)}) collective-permute-start(f32[128,128]{1,0:T(8,128)S(1)} %get-tuple-element.42), channel_id=1, source_target_pairs={{0,12},{1,13},{2,14},{3,15},{4,0},{5,1},{6,2},{7,3},{8,4},{9,5},{1... | collective-permute-start | bytes 196616 | tf_op jit(solution)/shard_map/ppermute | solution.py:25

commit v4 on v3

--- a/solution.py
+++ b/solution.py
@@ -129,7 +129,7 @@
 
 def pack_only_kernel(own, first, second, third, near):
     for s, shard in enumerate((own, first, second, third)):
-        near[s] = shard[...]
+        near[s] = shard[...].T
 
 
 def gram_kernel(shards, gram):
@@ -296,7 +296,7 @@
 
 def body(doc_tiles, tile_rows, tile_cols, tile_count, factor_h, factor_w):
     tiles = doc_tiles[0]
-    own = factor_h.T
+    own = factor_h
     shifted = [along_y(own, s) for s in (1, 2, 3)]
     plan = make_plan(tile_rows, tile_cols, tile_count, tiles)
     near, plan = lax.optimization_barrier((pack([own] + shifted), plan))

time: 76.7 us -> 75.6 us (0.986)
  waiting for transfers between devices: 15.5 us -> 11 us
  starting transfers between devices: 25.6 us -> 28.1 us
  Pallas kernels: 11.2 us -> 13.4 us
  local copies, waits for them, and re-layouts: 6.79 us -> 5.77 us
  blocking collectives: 16.9 us -> 16.1 us
    ppermute x6, waiting for transfers between devices: 11.7 us -> 7.17 us  [along_z(): lax.ppermute(x, 'doc', [(i, i // 4 * 4 + (i + step) % 4) for i in range(1...]
    ppermute x6, starting transfers between devices: 9.8 us -> 12.2 us  [along_z(): lax.ppermute(x, 'doc', [(i, i // 4 * 4 + (i + step) % 4) for i in range(1...]
    pallas_call x2, Pallas kernels: 6.6 us -> 8.63 us  [tile_products(): pl.pallas_call(functools.partial(products_kernel, half), out_shape=[jax.S...]
    unnamed x5 -> x6, local copies, waits for them, and re-layouts: 6.79 us -> 5.77 us
  transfers between devices with their start and end apart: 16 -> 16, of which waited for: 5 -> 5; matrix products, arithmetic and copies ran while one was open for 0% -> 0% of each run, Pallas kernels for 6% -> 7%
where the time goes in v4:
time: 75.6 us; the launch traced here: 75.2 us
  starting transfers between devices  28.1 us (37%)
  blocking collectives  16.1 us (21%)
  Pallas kernels  13.4 us (18%)
  waiting for transfers between devices  11 us (15%)
  local copies, waits for them, and re-layouts  5.77 us (8%)
  between operations  0.79 us (1%)
    all_to_all x1, blocking collectives, body(): shared = lax.all_to_all(squares.reshape(128, 1, 128), ('term', 'doc'), 0, 0)  16.1 us
    ppermute x6, starting transfers between devices, along_z(): lax.ppermute(x, 'doc', [(i, i // 4 * 4 + (i + step) % 4) for i in range(1...  12.2 us
    pallas_call x2, Pallas kernels, tile_products(): pl.pallas_call(functools.partial(products_kernel, half), out_shape=[jax.S...  8.63 us
    ppermute x6, starting transfers between devices, along_x(): return lax.ppermute(x, 'doc', [(i, (i + 4 * step) % 16) for i in range(16)])  8.55 us
    ppermute x6, waiting for transfers between devices, along_z(): lax.ppermute(x, 'doc', [(i, i // 4 * 4 + (i + step) % 4) for i in range(1...  7.17 us
    ppermute x3, starting transfers between devices, along_y(): return lax.ppermute(x, 'term', [(i, (i + 2 * step) % 8) for i in range(8)])  5.81 us
    unnamed x6, local copies, waits for them, and re-layouts  5.77 us
    ppermute x6, waiting for transfers between devices, along_x(): return lax.ppermute(x, 'doc', [(i, (i + 4 * step) % 16) for i in range(16)])  2.65 us
  transfers between devices with their start and end apart: 16, of which 5 were waited for; matrix products, arithmetic and copies ran while one was open for 0% of the time, Pallas kernels for 7%

profile of v4, /device:TPU:1, one launch (start us, length us, event | category | flops | bytes accessed | tf_op | source)
XLA Modules:
  0.0 75.2 jit_solution(14972214543665077410)
XLA Ops:
  0.0 2.1 %collective-permute-start = (bf16[128,512]{1,0:T(8,128)(2,1)}, bf16[128,512]{1,0:T(8,128)(2,1)S(1)}, u32[]{:S(2)}, u32[]{:S(2)}) collective-permute-start(bf16[128,512]{1,0:T(8,128)(2,1)} %own.1), channel_id=1, source_target_pairs={{0,32},{16,48},{32,64},{48,80},{64,96},{80,112},{96,0},{112,16},{1... | collective-permute-start | bytes 393224 | tf_op jit(solution)/shard_map/ppermute | solution.py:17
  2.1 2.6 %collective-permute-start.1 = (bf16[128,512]{1,0:T(8,128)(2,1)}, bf16[128,512]{1,0:T(8,128)(2,1)S(1)}, u32[]{:S(2)}, u32[]{:S(2)}) collective-permute-start(bf16[128,512]{1,0:T(8,128)(2,1)} %own.1), channel_id=1, source_target_pairs={{0,64},{16,80},{32,96},{48,112},{64,0},{80,16},{96,32},{112,48},{1... | collective-permute-start | bytes 393224 | tf_op jit(solution)/shard_map/ppermute | solution.py:17
  4.7 1.1 %collective-permute-start.2 = (bf16[128,512]{1,0:T(8,128)(2,1)}, bf16[128,512]{1,0:T(8,128)(2,1)S(1)}, u32[]{:S(2)}, u32[]{:S(2)}) collective-permute-start(bf16[128,512]{1,0:T(8,128)(2,1)} %own.1), channel_id=1, source_target_pairs={{0,96},{16,112},{32,0},{48,16},{64,32},{80,48},{96,64},{112,80},{1... | collective-permute-start | bytes 393224 | tf_op jit(solution)/shard_map/ppermute | solution.py:17
  6.5 5.8 %copy-done = bf16[1,512,128,128]{3,2,1,0:T(8,128)(2,1)S(1)} copy-done((bf16[1,512,128,128]{3,2,1,0:T(8,128)(2,1)S(1)}, bf16[1,512,128,128]{3,2,1,0:T(8,128)(2,1)}, u32[]{:S(2)}) %copy-start) | copy-done | bytes 16777240
  12.2 1.6 %shard_map.65.plan_in = s32[16,128]{1,0:T(8,128)S(1)} custom-call(s32[1,512]{1,0:T(1,128)} %rows_in.1, s32[1,512]{1,0:T(1,128)} %columns_in.1, s32[1,1]{1,0:T(1,128)S(6)} %copy.8.count, bf16[512,128,128]{2,1,0:T(8,128)(2,1)S(1)} %bitcast.5), custom_call_target="tpu_custom_call" | custom-call | flops 100000000 | bytes 100000 | tf_op jit(solution)/shard_map/pallas_call | solution.py:95
  14.1 1.6 %collective-permute-start.3 = (bf16[4,512,128]{2,1,0:T(8,128)(2,1)S(1)}, bf16[4,512,128]{2,1,0:T(8,128)(2,1)S(1)}, u32[]{:S(2)}, u32[]{:S(2)}) collective-permute-start(bf16[4,512,128]{2,1,0:T(8,128)(2,1)S(1)} %shard_map.64.shards.near), channel_id=1, source_target_pairs={{0,16},{16,0},{32,48},{48,32},{64,80},{80,64},{96,112},{112,96},{1... | collective-permute-start | bytes 1572872 | tf_op jit(solution)/shard_map/ppermute | solution.py:21
  16.0 1.2 %collective-permute-done.3.far = bf16[4,512,128]{2,1,0:T(8,128)(2,1)S(1)} collective-permute-done((bf16[4,512,128]{2,1,0:T(8,128)(2,1)S(1)}, bf16[4,512,128]{2,1,0:T(8,128)(2,1)S(1)}, u32[]{:S(2)}, u32[]{:S(2)}) %collective-permute-start.3) | collective-permute-done | bytes 524320 | tf_op jit(solution)/shard_map/ppermute | solution.py:21
  17.2 5.8 %shard_map.68 = (f32[512,128]{1,0:T(8,128)S(1)}, f32[512,128]{1,0:T(8,128)S(1)}, f32[512,128]{1,0:T(8,128)S(1)}, f32[512,128]{1,0:T(8,128)S(1)}) custom-call(s32[16,128]{1,0:T(8,128)S(1)} %shard_map.65.plan_in, bf16[4,512,128]{2,1,0:T(8,128)(2,1)S(1)} %shard_map.64.shards.near, bf16[4,512,128]{2,1,0:T(8,128)(2,1)S(1)} %collective-permute-done.3.far, ...), custom_call_target="tpu_custom_call" | custom-call | flops 1000000000 | bytes 10000000 | tf_op jit(solution)/shard_map/pallas_call | solution.py:201
  23.0 0.7 collective-permute-start.10
  23.7 2.8 %shard_map.67 = (f32[640,128]{1,0:T(8,128)S(1)}, f32[640,128]{1,0:T(8,128)S(1)}, f32[640,128]{1,0:T(8,128)S(1)}, f32[640,128]{1,0:T(8,128)S(1)}) custom-call(s32[16,128]{1,0:T(8,128)S(1)} %shard_map.65.plan_in, bf16[4,512,128]{2,1,0:T(8,128)(2,1)S(1)} %shard_map.64.shards.near, bf16[4,512,128]{2,1,0:T(8,128)(2,1)S(1)} %collective-permute-done.3.far, ...), custom_call_target="tpu_custom_call" | custom-call | flops 1000000000 | bytes 10000000 | tf_op jit(solution)/shard_map/pallas_call | solution.py:201
  27.2 2.0 %collective-permute-start.6 = (f32[640,128]{1,0:T(8,128)S(1)}, f32[640,128]{1,0:T(8,128)S(1)}, u32[]{:S(2)}, u32[]{:S(2)}) collective-permute-start(f32[640,128]{1,0:T(8,128)S(1)} %get-tuple-element.30), channel_id=1, source_target_pairs={{0,12},{1,13},{2,14},{3,15},{4,0},{5,1},{6,2},{7,3},{8,4},{9,5},{1... | collective-permute-start | bytes 983048 | tf_op jit(solution)/shard_map/ppermute | solution.py:25
  29.3 3.0 %collective-permute-start.11 = (f32[512,128]{1,0:T(8,128)S(1)}, f32[512,128]{1,0:T(8,128)S(1)}, u32[]{:S(2)}, u32[]{:S(2)}) collective-permute-start(f32[512,128]{1,0:T(8,128)S(1)} %get-tuple-element.37), channel_id=1, source_target_pairs={{0,2},{1,3},{2,0},{3,1},{4,6},{5,7},{6,4},{7,5},{8,10},{9,11},{10,... | collective-permute-start | bytes 786440 | tf_op jit(solution)/shard_map/ppermute | solution.py:29
  32.2 2.1 %collective-permute-start.12 = (f32[512,128]{1,0:T(8,128)S(1)}, f32[512,128]{1,0:T(8,128)S(1)}, u32[]{:S(2)}, u32[]{:S(2)}) collective-permute-start(f32[512,128]{1,0:T(8,128)S(1)} %get-tuple-element.38), channel_id=1, source_target_pairs={{0,3},{1,0},{2,1},{3,2},{4,7},{5,4},{6,5},{7,6},{8,11},{9,8},{10,9... | collective-permute-start | bytes 786440 | tf_op jit(solution)/shard_map/ppermute | solution.py:29
  34.3 1.7 %collective-permute-done.11.refs_2_ = f32[512,128]{1,0:T(8,128)S(1)} collective-permute-done((f32[512,128]{1,0:T(8,128)S(1)}, f32[512,128]{1,0:T(8,128)S(1)}, u32[]{:S(2)}, u32[]{:S(2)}) %collective-permute-start.11) | collective-permute-done | bytes 262176 | tf_op jit(solution)/shard_map/ppermute | solution.py:29
  36.0 5.4 %collective-permute-done.12.refs_3_ = f32[512,128]{1,0:T(8,128)S(1)} collective-permute-done((f32[512,128]{1,0:T(8,128)S(1)}, f32[512,128]{1,0:T(8,128)S(1)}, u32[]{:S(2)}, u32[]{:S(2)}) %collective-permute-start.12) | collective-permute-done | bytes 262176 | tf_op jit(solution)/shard_map/ppermute | solution.py:29
  41.5 3.4 %collective-permute-start.13 = (f32[128,128]{1,0:T(8,128)S(1)}, f32[128,128]{1,0:T(8,128)S(1)}, u32[]{:S(2)}, u32[]{:S(2)}) collective-permute-start(f32[128,128]{1,0:T(8,128)S(1)} %get-tuple-element.40), channel_id=1, source_target_pairs={{0,4},{1,5},{2,6},{3,7},{4,8},{5,9},{6,10},{7,11},{8,12},{9,13},{1... | collective-permute-start | bytes 196616 | tf_op jit(solution)/shard_map/ppermute | solution.py:25
  45.3 0.9 %collective-permute-start.7 = (f32[256,128]{1,0:T(8,128)S(1)}, f32[256,128]{1,0:T(8,128)S(1)}, u32[]{:S(2)}, u32[]{:S(2)}) collective-permute-start(f32[256,128]{1,0:T(8,128)S(1)} %get-tuple-element.33), channel_id=1, source_target_pairs={{0,1},{1,2},{2,3},{3,0},{4,5},{5,6},{6,7},{7,4},{8,9},{9,10},{10,1... | collective-permute-start | bytes 393224 | tf_op jit(solution)/shard_map/ppermute | solution.py:29
  46.2 3.6 %collective-permute-start.8 = (f32[256,128]{1,0:T(8,128)S(1)}, f32[256,128]{1,0:T(8,128)S(1)}, u32[]{:S(2)}, u32[]{:S(2)}) collective-permute-start(f32[256,128]{1,0:T(8,128)S(1)} %get-tuple-element.34), channel_id=1, source_target_pairs={{0,2},{1,3},{2,0},{3,1},{4,6},{5,7},{6,4},{7,5},{8,10},{9,11},{10,... | collective-permute-start | bytes 393224 | tf_op jit(solution)/shard_map/ppermute | solution.py:29
  49.8 2.0 %collective-permute-start.9 = (f32[256,128]{1,0:T(8,128)S(1)}, f32[256,128]{1,0:T(8,128)S(1)}, u32[]{:S(2)}, u32[]{:S(2)}) collective-permute-start(f32[256,128]{1,0:T(8,128)S(1)} %get-tuple-element.35), channel_id=1, source_target_pairs={{0,3},{1,0},{2,1},{3,2},{4,7},{5,4},{6,5},{7,6},{8,11},{9,8},{10,9... | collective-permute-start | bytes 393224 | tf_op jit(solution)/shard_map/ppermute | solution.py:29
  51.8 2.4 %collective-permute-start.15 = (f32[128,128]{1,0:T(8,128)S(1)}, f32[128,128]{1,0:T(8,128)S(1)}, u32[]{:S(2)}, u32[]{:S(2)}) collective-permute-start(f32[128,128]{1,0:T(8,128)S(1)} %get-tuple-element.42), channel_id=1, source_target_pairs={{0,12},{1,13},{2,14},{3,15},{4,0},{5,1},{6,2},{7,3},{8,4},{9,5},{1... | collective-permute-start | bytes 196616 | tf_op jit(solution)/shard_map/ppermute | solution.py:25
  54.2 2.4 %collective-permute-done.14.refs_6_ = f32[128,128]{1,0:T(8,128)S(1)} collective-permute-done((f32[128,128]{1,0:T(8,128)S(1)}, f32[128,128]{1,0:T(8,128)S(1)}, u32[]{:S(2)}, u32[]{:S(2)}) %collective-permute-start.14) | collective-permute-done | bytes 65568 | tf_op jit(solution)/shard_map/ppermute | solution.py:25
  56.6 1.8 %shard_map.71 = (f32[256,128]{1,0:T(8,128)S(1)}, f32[128,128]{1,0:T(8,128)S(1)}) custom-call(f32[256,128]{1,0:T(8,128)S(1)} %get-tuple-element.32.refs_0_, f32[256,128]{1,0:T(8,128)S(1)} %collective-permute-done.7.refs_1_, f32[256,128]{1,0:T(8,128)S(1)} %collective-permute-done.8.refs_2_, f32[256,128]{1,0:T(8,128)S(1)} %collective-permute-done.9.refs_3_, ...), custom_call_target="tpu_custom_call" | custom-call | tf_op jit(solution)/shard_map/pallas_call | solution.py:272
  58.4 16.1 %all_to_all.5 = f32[128,1,128]{2,1,0:T(1,128)S(1)} all-to-all(f32[128,1,128]{2,1,0:T(1,128)S(1)} %bitcast.9), channel_id=1, replica_groups=mesh['term'=8,'doc'=16] {'term','doc'}, dimensions={0} | all-to-all | bytes 131072 | tf_op jit(solution)/shard_map/all_to_all | solution.py:316
  74.5 0.7 shard_map.72
  (24 shorter events, 1.7 us)
Async XLA Ops:
  0.0 13.8 %collective-permute-start = (bf16[128,512]{1,0:T(8,128)(2,1)}, bf16[128,512]{1,0:T(8,128)(2,1)S(1)}, u32[]{:S(2)}, u32[]{:S(2)}) collective-permute-start(bf16[128,512]{1,0:T(8,128)(2,1)} %own.1), channel_id=1, source_target_pairs={{0,32},{16,48},{32,64},{48,80},{64,96},{80,112},{96,0},{112,16},{1... | collective-permute-start | bytes 393224 | tf_op jit(solution)/shard_map/ppermute | solution.py:17
  2.1 11.7 %collective-permute-start.1 = (bf16[128,512]{1,0:T(8,128)(2,1)}, bf16[128,512]{1,0:T(8,128)(2,1)S(1)}, u32[]{:S(2)}, u32[]{:S(2)}) collective-permute-start(bf16[128,512]{1,0:T(8,128)(2,1)} %own.1), channel_id=1, source_target_pairs={{0,64},{16,80},{32,96},{48,112},{64,0},{80,16},{96,32},{112,48},{1... | collective-permute-start | bytes 393224 | tf_op jit(solution)/shard_map/ppermute | solution.py:17
  4.7 9.1 %collective-permute-start.2 = (bf16[128,512]{1,0:T(8,128)(2,1)}, bf16[128,512]{1,0:T(8,128)(2,1)S(1)}, u32[]{:S(2)}, u32[]{:S(2)}) collective-permute-start(bf16[128,512]{1,0:T(8,128)(2,1)} %own.1), channel_id=1, source_target_pairs={{0,96},{16,112},{32,0},{48,16},{64,32},{80,48},{96,64},{112,80},{1... | collective-permute-start | bytes 393224 | tf_op jit(solution)/shard_map/ppermute | solution.py:17
  6.5 5.8 %copy-start = (bf16[1,512,128,128]{3,2,1,0:T(8,128)(2,1)S(1)}, bf16[1,512,128,128]{3,2,1,0:T(8,128)(2,1)}, u32[]{:S(2)}) copy-start(bf16[1,512,128,128]{3,2,1,0:T(8,128)(2,1)} %param.6) | copy-start | bytes 50331652
  12.2 1.6 %copy-start.2 = (bf16[128,512]{1,0:T(8,128)(2,1)S(1)}, bf16[128,512]{1,0:T(8,128)(2,1)}, u32[]{:S(2)}) copy-start(bf16[128,512]{1,0:T(8,128)(2,1)} %own.1) | copy-start | bytes 393220
  14.1 3.1 %collective-permute-start.3 = (bf16[4,512,128]{2,1,0:T(8,128)(2,1)S(1)}, bf16[4,512,128]{2,1,0:T(8,128)(2,1)S(1)}, u32[]{:S(2)}, u32[]{:S(2)}) collective-permute-start(bf16[4,512,128]{2,1,0:T(8,128)(2,1)S(1)} %shard_map.64.shards.near), channel_id=1, source_target_pairs={{0,16},{16,0},{32,48},{48,32},{64,80},{80,64},{96,112},{112,96},{1... | collective-permute-start | bytes 1572872 | tf_op jit(solution)/shard_map/ppermute | solution.py:21
  16.0 40.6 %copy-start.1 = (f32[256,128]{1,0:T(8,128)S(1)}, f32[256,128]{1,0:T(8,128)}, u32[]{:S(2)}) copy-start(f32[256,128]{1,0:T(8,128)} %refs_8_.1) | copy-start | bytes 393220
  23.0 9.2 %collective-permute-start.10 = (f32[512,128]{1,0:T(8,128)S(1)}, f32[512,128]{1,0:T(8,128)S(1)}, u32[]{:S(2)}, u32[]{:S(2)}) collective-permute-start(f32[512,128]{1,0:T(8,128)S(1)} %get-tuple-element.36), channel_id=1, source_target_pairs={{0,1},{1,2},{2,3},{3,0},{4,5},{5,6},{6,7},{7,4},{8,9},{9,10},{10,1... | collective-permute-start | bytes 786440 | tf_op jit(solution)/shard_map/ppermute | solution.py:29
  26.5 18.4 %collective-permute-start.4 = (f32[640,128]{1,0:T(8,128)S(1)}, f32[640,128]{1,0:T(8,128)S(1)}, u32[]{:S(2)}, u32[]{:S(2)}) collective-permute-start(f32[640,128]{1,0:T(8,128)S(1)} %get-tuple-element.28), channel_id=1, source_target_pairs={{0,4},{1,5},{2,6},{3,7},{4,8},{5,9},{6,10},{7,11},{8,12},{9,13},{1... | collective-permute-start | bytes 983048 | tf_op jit(solution)/shard_map/ppermute | solution.py:25
  26.6 18.3 %collective-permute-start.5 = (f32[640,128]{1,0:T(8,128)S(1)}, f32[640,128]{1,0:T(8,128)S(1)}, u32[]{:S(2)}, u32[]{:S(2)}) collective-permute-start(f32[640,128]{1,0:T(8,128)S(1)} %get-tuple-element.29), channel_id=1, source_target_pairs={{0,8},{1,9},{2,10},{3,11},{4,12},{5,13},{6,14},{7,15},{8,0},{9,1},... | collective-permute-start | bytes 983048 | tf_op jit(solution)/shard_map/ppermute | solution.py:25
  27.2 17.9 %collective-permute-start.6 = (f32[640,128]{1,0:T(8,128)S(1)}, f32[640,128]{1,0:T(8,128)S(1)}, u32[]{:S(2)}, u32[]{:S(2)}) collective-permute-start(f32[640,128]{1,0:T(8,128)S(1)} %get-tuple-element.30), channel_id=1, source_target_pairs={{0,12},{1,13},{2,14},{3,15},{4,0},{5,1},{6,2},{7,3},{8,4},{9,5},{1... | collective-permute-start | bytes 983048 | tf_op jit(solution)/shard_map/ppermute | solution.py:25
  29.3 6.7 %collective-permute-start.11 = (f32[512,128]{1,0:T(8,128)S(1)}, f32[512,128]{1,0:T(8,128)S(1)}, u32[]{:S(2)}, u32[]{:S(2)}) collective-permute-start(f32[512,128]{1,0:T(8,128)S(1)} %get-tuple-element.37), channel_id=1, source_target_pairs={{0,2},{1,3},{2,0},{3,1},{4,6},{5,7},{6,4},{7,5},{8,10},{9,11},{10,... | collective-permute-start | bytes 786440 | tf_op jit(solution)/shard_map/ppermute | solution.py:29
  32.2 9.2 %collective-permute-start.12 = (f32[512,128]{1,0:T(8,128)S(1)}, f32[512,128]{1,0:T(8,128)S(1)}, u32[]{:S(2)}, u32[]{:S(2)}) collective-permute-start(f32[512,128]{1,0:T(8,128)S(1)} %get-tuple-element.38), channel_id=1, source_target_pairs={{0,3},{1,0},{2,1},{3,2},{4,7},{5,4},{6,5},{7,6},{8,11},{9,8},{10,9... | collective-permute-start | bytes 786440 | tf_op jit(solution)/shard_map/ppermute | solution.py:29
  41.5 10.2 %collective-permute-start.13 = (f32[128,128]{1,0:T(8,128)S(1)}, f32[128,128]{1,0:T(8,128)S(1)}, u32[]{:S(2)}, u32[]{:S(2)}) collective-permute-start(f32[128,128]{1,0:T(8,128)S(1)} %get-tuple-element.40), channel_id=1, source_target_pairs={{0,4},{1,5},{2,6},{3,7},{4,8},{5,9},{6,10},{7,11},{8,12},{9,13},{1... | collective-permute-start | bytes 196616 | tf_op jit(solution)/shard_map/ppermute | solution.py:25
  45.3 11.3 %collective-permute-start.7 = (f32[256,128]{1,0:T(8,128)S(1)}, f32[256,128]{1,0:T(8,128)S(1)}, u32[]{:S(2)}, u32[]{:S(2)}) collective-permute-start(f32[256,128]{1,0:T(8,128)S(1)} %get-tuple-element.33), channel_id=1, source_target_pairs={{0,1},{1,2},{2,3},{3,0},{4,5},{5,6},{6,7},{7,4},{8,9},{9,10},{10,1... | collective-permute-start | bytes 393224 | tf_op jit(solution)/shard_map/ppermute | solution.py:29
  46.2 10.4 %collective-permute-start.8 = (f32[256,128]{1,0:T(8,128)S(1)}, f32[256,128]{1,0:T(8,128)S(1)}, u32[]{:S(2)}, u32[]{:S(2)}) collective-permute-start(f32[256,128]{1,0:T(8,128)S(1)} %get-tuple-element.34), channel_id=1, source_target_pairs={{0,2},{1,3},{2,0},{3,1},{4,6},{5,7},{6,4},{7,5},{8,10},{9,11},{10,... | collective-permute-start | bytes 393224 | tf_op jit(solution)/shard_map/ppermute | solution.py:29
  49.8 6.8 %collective-permute-start.9 = (f32[256,128]{1,0:T(8,128)S(1)}, f32[256,128]{1,0:T(8,128)S(1)}, u32[]{:S(2)}, u32[]{:S(2)}) collective-permute-start(f32[256,128]{1,0:T(8,128)S(1)} %get-tuple-element.35), channel_id=1, source_target_pairs={{0,3},{1,0},{2,1},{3,2},{4,7},{5,4},{6,5},{7,6},{8,11},{9,8},{10,9... | collective-permute-start | bytes 393224 | tf_op jit(solution)/shard_map/ppermute | solution.py:29
  51.7 4.8 %collective-permute-start.14 = (f32[128,128]{1,0:T(8,128)S(1)}, f32[128,128]{1,0:T(8,128)S(1)}, u32[]{:S(2)}, u32[]{:S(2)}) collective-permute-start(f32[128,128]{1,0:T(8,128)S(1)} %get-tuple-element.41), channel_id=1, source_target_pairs={{0,8},{1,9},{2,10},{3,11},{4,12},{5,13},{6,14},{7,15},{8,0},{9,1},... | collective-permute-start | bytes 196616 | tf_op jit(solution)/shard_map/ppermute | solution.py:25
  51.8 4.8 %collective-permute-start.15 = (f32[128,128]{1,0:T(8,128)S(1)}, f32[128,128]{1,0:T(8,128)S(1)}, u32[]{:S(2)}, u32[]{:S(2)}) collective-permute-start(f32[128,128]{1,0:T(8,128)S(1)} %get-tuple-element.42), channel_id=1, source_target_pairs={{0,12},{1,13},{2,14},{3,15},{4,0},{5,1},{6,2},{7,3},{8,4},{9,5},{1... | collective-permute-start | bytes 196616 | tf_op jit(solution)/shard_map/ppermute | solution.py:25
